TPU v7x, 128 devices: a whole 4x4x4 slice. The times are simulated.
128 devices in a mesh: grp: 16 (over x_hi, y, core), head: 8 (over x_lo, z).
Axes of the slice: x: 4 (x_hi: 2, x_lo: 2; x = x_hi * 2 + x_lo), y: 4, z: 4, core: 2. Of those that a mesh axis runs over, the one named last changes fastest.
Arguments:
- query: bfloat16 [512, 8192], P('grp', 'head'), may hold values from -160 to 160
- new_key: bfloat16 [512, 1024], P('grp', 'head'), may hold values from -6 to 6
- new_value: bfloat16 [512, 1024], P('grp', 'head'), may hold values from -6 to 6
- key_cache: bfloat16 [512, 8, 1024, 128], P('grp', 'head'), may hold values from -6 to 6
- value_cache: bfloat16 [512, 8, 1024, 128], P('grp', 'head'), may hold values from -6 to 6
- lengths: int32 [512], P('grp'), may hold values from 1 to 1024, 262144 in all
- slot_row: int32 [512], replicated, may hold values from 0 to 511, each once
- resid: bfloat16 [512, 8192], P(None, 'grp'), may hold values from -10 to 10
- out_weight: bfloat16 [8192, 8192], P('head', 'grp'), may hold values from -0.5 to 0.5
- norm_gain: bfloat16 [8192], P('grp'), may hold values from 0.5 to 1.5
- gate_weight: bfloat16 [8192, 28672], P(None, ('grp', 'head')), may hold values from -0.0625 to 0.0625
- up_weight: bfloat16 [8192, 28672], P(None, ('grp', 'head')), may hold values from -0.0625 to 0.0625
- down_weight: bfloat16 [28672, 8192], P(('grp', 'head')), may hold values from -0.125 to 0.125
Outputs:
- residual_out: bfloat16 [512, 8192], P(None, ('grp', 'head'))
- layer_out: bfloat16 [512, 8192], P(None, ('grp', 'head'))
Inputs may be any that keep to these rules, and one draw needn't show every extreme that they name: `lengths`: each row attends to its cache slots below its length and to its own new key. `slot_row`: A permutation of the rows.
All inputs are finite; a program needn't handle non-finite values. No bound on the sum of `lengths` on one device may be relied on, other than what follows from the above.
Results may differ from a plain program's by a relative error of at most 0.015.
Values may be sent and summed in bfloat16 or wider, within the bound.
A program may use at most 128 MiB of HBM per device.

v0:
```python
import jax
import jax.numpy as jnp
from jax import lax
from jax.sharding import PartitionSpec as P

D = 8192
HQ = 64
KVH = 8


def attend_local(query, new_key, new_value, key_cache, value_cache, lengths):
    rows_here, kv_here, cache_len, head_size = key_cache.shape
    per_kv = HQ // KVH
    query_heads = query.reshape(rows_here, kv_here, per_kv, head_size)
    score_scale = head_size ** (-0.5)
    scores = (
        jnp.einsum("rjqd,rjpd->rjqp", query_heads, key_cache, preferred_element_type=jnp.float32)
        * score_scale
    )
    own_score = (
        jnp.einsum(
            "rjqd,rjd->rjq",
            query_heads,
            new_key.reshape(rows_here, kv_here, head_size),
            preferred_element_type=jnp.float32,
        )
        * score_scale
    )
    live_mask = (jnp.arange(cache_len, dtype=jnp.int32)[None, :] < lengths[:, None])[
        :, None, None, :
    ]
    scores = jnp.where(live_mask, scores, -1e30)
    row_top = jnp.maximum(jnp.max(scores, axis=3), own_score)
    exp_scores = jnp.where(live_mask, jnp.exp(scores - row_top[..., None]), 0.0)
    exp_own = jnp.exp(own_score - row_top)
    weight_sum = jnp.sum(exp_scores, axis=3) + exp_own
    weights = (exp_scores / weight_sum[..., None]).astype(jnp.bfloat16)
    own_weight = (exp_own / weight_sum).astype(jnp.bfloat16)
    mixed_values = jnp.einsum(
        "rjqp,rjpd->rjqd", weights, value_cache, preferred_element_type=jnp.float32
    )
    own_values = new_value.reshape(rows_here, kv_here, 1, head_size).astype(jnp.float32)
    mixed_values = mixed_values + own_weight.astype(jnp.float32)[..., None] * own_values
    return mixed_values.reshape(rows_here, kv_here * per_kv * head_size).astype(jnp.bfloat16)


def layer_rows(
    attended,
    slot_index,
    slot_row,
    resid,
    out_weight,
    norm_gain,
    gate_weight,
    up_weight,
    down_weight,
):
    partial_proj = jnp.dot(
        lax.all_gather(attended, "grp", axis=0, tiled=True),
        out_weight,
        preferred_element_type=jnp.float32,
    )
    resid_rows = resid[slot_row[slot_index]]
    summed = lax.psum(partial_proj, "head")
    stream = resid_rows.astype(jnp.float32) + summed
    sum_squares = lax.psum(jnp.sum(stream * stream, axis=1), "grp")
    normed = (
        stream * lax.rsqrt(sum_squares / D + 1e-05)[:, None] * norm_gain.astype(jnp.float32)
    ).astype(jnp.bfloat16)
    block_cols = lax.all_gather(normed, "grp", axis=1, tiled=True)
    gate_acc = jnp.dot(block_cols, gate_weight, preferred_element_type=jnp.float32)
    up_acc = jnp.dot(block_cols, up_weight, preferred_element_type=jnp.float32)
    share_width = stream.shape[1] // lax.axis_size("head")
    residual_rows = lax.dynamic_slice_in_dim(
        stream, lax.axis_index("head") * share_width, share_width, 1
    ).astype(jnp.bfloat16)
    hidden = (jax.nn.silu(gate_acc) * up_acc).astype(jnp.bfloat16)
    ffn_terms = jnp.dot(hidden, down_weight, preferred_element_type=jnp.float32)
    output_rows = lax.psum_scatter(
        ffn_terms, ("grp", "head"), scatter_dimension=1, tiled=True
    ).astype(jnp.bfloat16)
    return (residual_rows, output_rows)


def per_device(
    query,
    new_key,
    new_value,
    key_cache,
    value_cache,
    lengths,
    slot_row,
    resid,
    out_weight,
    norm_gain,
    gate_weight,
    up_weight,
    down_weight,
):
    rows_here = query.shape[0]
    group_count = lax.axis_size("grp")
    total_rows = rows_here * group_count
    inverse = (
        jnp.zeros((total_rows,), jnp.int32)
        .at[slot_row]
        .set(jnp.arange(total_rows, dtype=jnp.int32))
    )
    attended = attend_local(query, new_key, new_value, key_cache, value_cache, lengths)
    group_starts = jnp.arange(group_count, dtype=jnp.int32)[:, None] * rows_here
    slot_index = (group_starts + jnp.arange(rows_here, dtype=jnp.int32)[None, :]).reshape(-1)
    residual_slots, layer_slots = layer_rows(
        attended,
        slot_index,
        slot_row,
        resid,
        out_weight,
        norm_gain,
        gate_weight,
        up_weight,
        down_weight,
    )
    return (residual_slots[inverse], layer_slots[inverse])


def solution(mesh):
    placed = (
        P("grp", "head"),
        P("grp", "head"),
        P("grp", "head"),
        P("grp", "head", None, None),
        P("grp", "head", None, None),
        P("grp"),
        P(),
        P(None, "grp"),
        P("head", "grp"),
        P("grp"),
        P(None, ("grp", "head")),
        P(None, ("grp", "head")),
        P(("grp", "head"), None),
    )
    return jax.shard_map(
        per_device,
        mesh=mesh,
        in_specs=placed,
        out_specs=(P(None, ("grp", "head")), P(None, ("grp", "head"))),
        check_vma=False,
    )
```

profile of v0, /device:TPU:1, one launch (start us, length us, event | category | flops | bytes accessed | tf_op | source)
XLA Modules:
  0.0 941.3 jit_solution(14770041832936248734)
XLA Ops:
  7.2 0.0 copy-start
  7.2 0.0 all-gather.3.cloned.1.call-start
  7.2 0.0 copy-start.3
  7.2 0.9 convert_element_type.44
  8.1 1.0 iota_compare_fusion
  9.0 1.2 copy.23
  10.2 0.8 fusion.29
  11.1 5.7 fusion.37
  16.8 0.0 copy-start.4
  16.8 0.0 copy-start.1
  16.8 0.4 fusion.17
  17.2 0.0 copy-start.2
  17.2 0.0 copy-done.3
  17.3 1.3 fusion.14
  18.5 0.7 copy.28
  19.2 0.0 all-gather.3.cloned.1.call-update
  19.2 0.0 all-reduce.2.cloned.1.call-start
  19.3 48.5 %all-gather.3.cloned.1.call-done = bf16[512,1024]{1,0:T(8,128)(2,1)} async-done(((bf16[32,1024]{1,0:T(8,128)(2,1)}), bf16[512,1024]{1,0:T(8,128)(2,1)}) %all-gather.3.cloned.1.call-update) | async-done | bytes 1048592 | tf_op jit(solution)/shard_map/all_gather | solution.py:59
  67.7 0.0 copy-done
  67.7 2.9 fusion.38
  70.7 0.0 all-reduce.2.cloned.1.call-update
  70.7 0.0 all-gather.5.cloned.1.call-start
  70.7 0.0 copy-done.4
  70.8 0.1 iota_add_fusion
  70.8 0.1 add.84
  70.9 0.0 copy-done.1
  70.9 3.5 gather_fusion
  74.5 0.0 copy-done.2
  74.5 2.0 gather_fusion.1
  76.5 65.0 %all-reduce.2.cloned.1.call-done = f32[512,512]{1,0:T(8,128)} async-done(((f32[512,512]{1,0:T(8,128)}), f32[512,512]{1,0:T(8,128)}) %all-reduce.2.cloned.1.call-update) | async-done | bytes 1048592 | tf_op jit(solution)/shard_map/psum | solution.py:64
  141.5 1.5 multiply_reduce_fusion
  142.9 38.3 %psum.15 = f32[512]{0:T(512)S(1)} all-reduce(f32[512]{0:T(512)S(1)} %get-tuple-element.6), channel_id=1, replica_groups=mesh['grp'=16,'head'=8] {'grp'}, use_global_device_ids=true, to_apply=%region_5.6 | all-reduce | flops 512 | bytes 4096 | tf_op jit(solution)/shard_map/psum | solution.py:66
  181.2 0.9 multiply_convert_fusion
  182.1 0.0 all-gather.5.cloned.1.call-update
  182.2 0.2 reduce-scatter.2.cloned.1.call-start
  182.4 74.3 %all-gather.5.cloned.1.call-done = bf16[512,8192]{1,0:T(8,128)(2,1)} async-done(((bf16[512,512]{1,0:T(8,128)(2,1)}), bf16[512,8192]{1,0:T(8,128)(2,1)}) %all-gather.5.cloned.1.call-update) | async-done | bytes 8388624 | tf_op jit(solution)/shard_map/all_gather | solution.py:70
  256.7 7.1 fusion.39
  263.8 16.2 %fusion.18 = f32[512,8192]{0,1:T(8,128)} fusion(bf16[224,8192]{1,0:T(8,128)(2,1)} %param.25, bf16[512,8192]{1,0:T(8,128)(2,1)} %all-gather.5.cloned.1.call-done, bf16[8192,224]{0,1:T(8,128)(2,1)} %param.24, f32[512,224]{0,1:T(8,128)S(1)} %fusion.39), kind=kOutput, calls=%fused_computation.21 | convolution fusion | flops 3758784512 | bytes 32964608 | tf_op jit(solution)/shard_map/dot_general | solution.py:78
  280.1 0.0 reduce-scatter.2.cloned.1.call-update
  280.1 2.4 scatter_custom_fusion
  282.6 0.1 dynamic-slice_convert_fusion
  282.7 1.3 gather_fusion.2
  284.1 0.7 copy.19
  284.8 646.9 %reduce-scatter.2.cloned.1.call-done = f32[512,64]{0,1:T(8,128)} async-done(((f32[512,8192]{0,1:T(8,128)}), f32[512,64]{0,1:T(8,128)}) %reduce-scatter.2.cloned.1.call-update) | async-done | bytes 131088 | tf_op jit(solution)/shard_map/reduce_scatter | solution.py:79
  931.7 0.9 convert_element_type.51
  932.6 0.1 copy.18
  932.7 1.3 gather_fusion.3
  934.1 0.7 copy.20
  (13 shorter events, 0.1 us)
Async XLA Ops:
  7.2 60.6 %copy-start = (bf16[1024,512]{1,0:T(8,128)(2,1)S(1)}, bf16[1024,512]{1,0:T(8,128)(2,1)}, u32[]{:S(2)}) copy-start(bf16[1024,512]{1,0:T(8,128)(2,1)} %param.21) | copy-start | bytes 3145732
  7.2 60.6 %all-gather.3.cloned.1.call-start = ((), (), s32[]{:S(2)}) async-start(), calls=%async_computation.1 | async-start | bytes 1114112 | tf_op jit(solution)/shard_map/all_gather | solution.py:59
  7.2 10.0 %copy-start.3 = (bf16[32,1,1024,128]{3,2,1,0:T(8,128)(2,1)S(1)}, bf16[32,1,1024,128]{3,2,1,0:T(8,128)(2,1)}, u32[]{:S(2)}) copy-start(bf16[32,1,1024,128]{3,2,1,0:T(8,128)(2,1)} %param.17) | copy-start | bytes 25165828
  16.8 53.9 %copy-start.4 = (bf16[512]{0:T(512)(128)(2,1)S(1)}, bf16[512]{0:T(512)(128)(2,1)}, u32[]{:S(2)}) copy-start(bf16[512]{0:T(512)(128)(2,1)} %param.22) | copy-start | bytes 3076
  16.8 54.1 %copy-start.1 = (s32[512]{0:T(512)S(1)}, s32[512]{0:T(512)}, u32[]{:S(2)}) copy-start(s32[512]{0:T(512)} %param.19) | copy-start | bytes 6148
  17.2 57.3 %copy-start.2 = (bf16[512,512]{1,0:T(8,128)(2,1)S(1)}, bf16[512,512]{1,0:T(8,128)(2,1)}, u32[]{:S(2)}) copy-start(bf16[512,512]{1,0:T(8,128)(2,1)} %param.20) | copy-start | bytes 1572868
  19.2 122.2 %all-reduce.2.cloned.1.call-start = ((), (), s32[]{:S(2)}) async-start(), calls=%async_computation.2 | async-start | bytes 2097152 | tf_op jit(solution)/shard_map/psum | solution.py:64
  70.7 186.0 %all-gather.5.cloned.1.call-start = ((), (), s32[]{:S(2)}) async-start(), calls=%async_computation.3 | async-start | bytes 8912896 | tf_op jit(solution)/shard_map/all_gather | solution.py:70
  182.2 749.5 %reduce-scatter.2.cloned.1.call-start = ((), (), s32[]{:S(2)}) async-start(), calls=%async_computation.4 | async-start | bytes 16908288 | tf_op jit(solution)/shard_map/reduce_scatter | solution.py:79
Sparse Core Ops, SparseCore 0:
  19.3 48.3 all-gather.2
  70.8 70.6 all-reduce.1
  182.3 74.3 all-gather.4
  280.2 651.3 reduce-scatter.1
where the time goes:
time: 957 us; the launch traced here: 941 us
  waiting for transfers between devices  835 us (87%)
  blocking collectives  38.3 us (4%)
  matrix products  34.1 us (4%)
  local copies, waits for them, and re-layouts  14.2 us (1%)
  between operations  14 us (1%)
    reduce_scatter x1, waiting for transfers between devices, layer_rows(): lax.psum_scatter(ffn_terms, ('grp', 'head'), scatter_dimension=1, tiled=T...  647 us
    all_gather x1, waiting for transfers between devices, layer_rows(): block_cols = lax.all_gather(normed, 'grp', axis=1, tiled=True)  74.3 us
    psum x1, waiting for transfers between devices, layer_rows(): summed = lax.psum(partial_proj, 'head')  65 us
    all_gather x1, waiting for transfers between devices, layer_rows(): lax.all_gather(attended, 'grp', axis=0, tiled=True)  48.5 us
    psum x1, blocking collectives, layer_rows(): sum_squares = lax.psum(jnp.sum(stream * stream, axis=1), 'grp')  38.3 us
  transfers between devices with their start and end apart: 4, of which 4 were waited for; matrix products, arithmetic and copies ran while one was open for 1% of the time, Pallas kernels for 0%

commit v1 on v0

v1 whole, which is shorter than its diff:
```python
import jax
import jax.numpy as jnp
from jax import lax
from jax.experimental import pallas as pl
from jax.experimental.pallas import tpu as pltpu
from jax.sharding import PartitionSpec as P

D = 8192
HQ = 64
KVH = 8
HID = 224
MESH = pl.DeviceIdType.MESH
BF16 = jnp.bfloat16
F32 = jnp.float32

GATHER_LANES = ((0, 384), (384, 384), (768, 256))
GATHER_ORDER = ("xzy", "yxz", "zyx")
SCATTER_ROWS = ((0, 96), (96, 96), (192, 64))
SCATTER_ORDER = ("yzx", "zxy", "xyz")


def attend_local(query, new_key, new_value, key_cache, value_cache, lengths):
    rows_here, kv_here, cache_len, head_size = key_cache.shape
    per_kv = HQ // KVH
    query_heads = query.reshape(rows_here, kv_here, per_kv, head_size)
    score_scale = head_size ** (-0.5)
    scores = (
        jnp.einsum("rjqd,rjpd->rjqp", query_heads, key_cache, preferred_element_type=jnp.float32)
        * score_scale
    )
    own_score = (
        jnp.einsum(
            "rjqd,rjd->rjq",
            query_heads,
            new_key.reshape(rows_here, kv_here, head_size),
            preferred_element_type=jnp.float32,
        )
        * score_scale
    )
    live_mask = (jnp.arange(cache_len, dtype=jnp.int32)[None, :] < lengths[:, None])[
        :, None, None, :
    ]
    scores = jnp.where(live_mask, scores, -1e30)
    row_top = jnp.maximum(jnp.max(scores, axis=3), own_score)
    exp_scores = jnp.where(live_mask, jnp.exp(scores - row_top[..., None]), 0.0)
    exp_own = jnp.exp(own_score - row_top)
    weight_sum = jnp.sum(exp_scores, axis=3) + exp_own
    weights = (exp_scores / weight_sum[..., None]).astype(jnp.bfloat16)
    own_weight = (exp_own / weight_sum).astype(jnp.bfloat16)
    mixed_values = jnp.einsum(
        "rjqp,rjpd->rjqd", weights, value_cache, preferred_element_type=jnp.float32
    )
    own_values = new_value.reshape(rows_here, kv_here, 1, head_size).astype(jnp.float32)
    mixed_values = mixed_values + own_weight.astype(jnp.float32)[..., None] * own_values
    return mixed_values.reshape(rows_here, kv_here * per_kv * head_size).astype(jnp.bfloat16)


def device_at(x, y, z, c):
    return ((x // 2) * 8 + y * 2 + c, (x % 2) * 4 + z)


def block_index(where):
    x, y, z = where["x"], where["y"], where["z"]
    if x is None:
        xl, xh = slice(None), slice(None)
    else:
        xl, xh = x % 2, x // 2
    return (xl, slice(None) if z is None else z, xh, slice(None) if y is None else y)


def kept_index(where, kept):
    index = ()
    if "x" in kept:
        index += (where["x"] % 2,)
    if "z" in kept:
        index += (where["z"],)
    if "x" in kept:
        index += (where["x"] // 2,)
    if "y" in kept:
        index += (where["y"],)
    return index


def kept_shape(kept):
    shape = ()
    if "x" in kept:
        shape += (2,)
    if "z" in kept:
        shape += (4,)
    if "x" in kept:
        shape += (2,)
    if "y" in kept:
        shape += (4,)
    return shape


def layer_kernel(
    att, gain, slots, resid, out_w, gate_w, up_w, down_w,
    res_out, lay_out,
    gains, got_att, resid_own, resid_sib, ow_own, ow_sib,
    gate_own, gate_sib, up_own, up_sib, down_own, down_sib,
    proj, proj_got, xs, ys, acc_go, acc_gs, acc_uo, acc_us, square,
    perm, slot_col, hid_own, hid_sib, res_z, lay_z, res_rows,
    *rest,
):
    landing = [[rest[k * 3 + s] for s in range(3)] for k in range(3)]
    (load_sem, swap_s, swap_r, att_s, att_r, gain_s, gain_r, proj_s, proj_r,
     ga_s, ga_r, sc_s, sc_r, fin_s, fin_r) = rest[9:]

    g = lax.axis_index("grp")
    h = lax.axis_index("head")
    xh, y, c = g // 8, (g // 2) % 4, g % 2
    xl, z = h // 4, h % 4
    me = {"x": xh * 2 + xl, "y": y, "z": z}

    def on_axis(axis, step):
        place = dict(me)
        place[axis] = (me[axis] + step) % 4
        return place

    def at(place, core):
        return device_at(place["x"], place["y"], place["z"], core)

    sibling = at(me, 1 - c)
    loads = []
    for i, (src, dst) in enumerate(
        ((out_w, ow_own), (resid, resid_own), (gate_w, gate_own), (up_w, up_own), (down_w, down_own))
    ):
        copy = pltpu.make_async_copy(src, dst, load_sem.at[i])
        copy.start()
        loads.append(copy)

    barrier = pltpu.get_barrier_semaphore()
    partners = []
    for i in range(1, 16):
        partners.append(((g + i) % 16, h))
    for i in range(1, 8):
        partners.append((g, (h + i) % 8))
    partners.append(((g + 8) % 16, (h + 4) % 8))
    for partner in partners:
        pl.semaphore_signal(barrier, inc=1, device_id=partner, device_id_type=MESH)
    pl.semaphore_wait(barrier, len(partners))

    att_copies = []
    for i in range(1, 8):
        xy = (xh * 4 + y + i) % 8
        copy = pltpu.make_async_remote_copy(
            src_ref=att,
            dst_ref=got_att.at[xh * 4 + y],
            send_sem=att_s.at[i - 1],
            recv_sem=att_r.at[i - 1],
            device_id=((xy // 4) * 8 + (xy % 4) * 2 + c, h),
            device_id_type=MESH,
        )
        copy.start()
        att_copies.append(copy)
    got_att[xh * 4 + y] = att[...]
    swaps = []
    for i, (src, dst) in enumerate(
        ((out_w, ow_sib), (resid, resid_sib), (gate_w, gate_sib), (up_w, up_sib), (down_w, down_sib))
    ):
        copy = pltpu.make_async_remote_copy(
            src_ref=src, dst_ref=dst, send_sem=swap_s.at[i], recv_sem=swap_r.at[i],
            device_id=sibling, device_id_type=MESH,
        )
        copy.start()
        swaps.append(copy)
    gain_copies = []
    for i in range(1, 16):
        copy = pltpu.make_async_remote_copy(
            src_ref=gain,
            dst_ref=gains.at[g],
            send_sem=gain_s.at[i - 1],
            recv_sem=gain_r.at[i - 1],
            device_id=((g + i) % 16, h),
            device_id_type=MESH,
        )
        copy.start()
        gain_copies.append(copy)
    gains[g] = gain[...]

    slot_line = slots[0:1, :]
    for t in range(4):
        tile = jnp.broadcast_to(slot_line[:, t * 128:(t + 1) * 128].astype(F32), (128, 128))
        slot_col[t * 128:(t + 1) * 128, :] = tile.T
        batch = lax.broadcasted_iota(jnp.int32, (128, 512), 0) + t * 128
        perm[t * 128:(t + 1) * 128, :] = jnp.where(batch == slot_line, 1.0, 0.0).astype(BF16)
    square[...] = jnp.zeros_like(square)
    acc_go[...] = jnp.zeros_like(acc_go)
    acc_gs[...] = jnp.zeros_like(acc_gs)
    acc_uo[...] = jnp.zeros_like(acc_uo)
    acc_us[...] = jnp.zeros_like(acc_us)

    loads[1].wait()
    swaps[1].wait()
    my_slots = slot_col[pl.ds(pl.multiple_of((2 * h + c) * 32, 32), 32), :]
    lane = lax.broadcasted_iota(jnp.int32, (32, 128), 1).astype(F32)
    pick = jnp.concatenate(
        [jnp.where(my_slots == lane + 128.0 * t, 1.0, 0.0).astype(BF16) for t in range(4)], axis=1
    )

    @pl.when(c == 0)
    def _():
        res_rows[:, 0:512] = jnp.dot(pick, resid_own[...], preferred_element_type=F32)
        res_rows[:, 512:1024] = jnp.dot(pick, resid_sib[...], preferred_element_type=F32)

    @pl.when(c == 1)
    def _():
        res_rows[:, 0:512] = jnp.dot(pick, resid_sib[...], preferred_element_type=F32)
        res_rows[:, 512:1024] = jnp.dot(pick, resid_own[...], preferred_element_type=F32)

    loads[0].wait()
    swaps[0].wait()
    for copy in att_copies:
        copy.wait()
    rows = got_att[...].reshape(256, 1024)
    own_part = jnp.dot(rows, ow_own[...], preferred_element_type=F32).astype(BF16)
    sib_part = jnp.dot(rows, ow_sib[...], preferred_element_type=F32).astype(BF16)
    proj[:, :, pl.ds(pl.multiple_of(c * 512, 512), 512)] = own_part.reshape(8, 32, 512)
    proj[:, :, pl.ds(pl.multiple_of((1 - c) * 512, 512), 512)] = sib_part.reshape(8, 32, 512)
    proj_copies = []
    for i in range(1, 8):
        head = (h + i) % 8
        copy = pltpu.make_async_remote_copy(
            src_ref=proj.at[head],
            dst_ref=proj_got.at[i - 1],
            send_sem=proj_s.at[i - 1],
            recv_sem=proj_r.at[i - 1],
            device_id=(g, head),
            device_id_type=MESH,
        )
        copy.start()
        proj_copies.append(copy)
    total = res_rows[...] + proj[h].astype(F32)
    for i in range(7):
        proj_copies[i].wait()
        total = total + proj_got[i].astype(F32)
    mine = block_index(me)
    xs[mine] = total.astype(BF16)

    def gather_stage(k, s):
        order = GATHER_ORDER[k]
        start, width = GATHER_LANES[k]
        lanes = pl.ds(start, width)
        done = order[:s]
        src_place = {a: (None if a in done else me[a]) for a in "xyz"}
        src = xs.at[(*block_index(src_place), slice(None), lanes)]
        copies = []
        for d in range(1, 4):
            copy = pltpu.make_async_remote_copy(
                src_ref=src, dst_ref=src,
                send_sem=ga_s.at[k, s, d - 1], recv_sem=ga_r.at[k, s, d - 1],
                device_id=at(on_axis(order[s], d), c), device_id_type=MESH,
            )
            copy.start()
            copies.append(copy)
        return copies

    def gather_wait(k, s, copies):
        order = GATHER_ORDER[k]
        start, width = GATHER_LANES[k]
        lanes = pl.ds(start, width)
        done = order[:s]
        for d in range(1, 4):
            place = on_axis(order[s], 4 - d)
            place = {a: (None if a in done else place[a]) for a in "xyz"}
            dst = xs.at[(*block_index(place), slice(None), lanes)]
            pltpu.make_async_remote_copy(
                src_ref=dst, dst_ref=dst,
                send_sem=ga_s.at[k, s, d - 1], recv_sem=ga_r.at[k, s, d - 1],
                device_id=at(on_axis(order[s], d), c), device_id_type=MESH,
            ).wait_recv()

    stages = [[None] * 3 for _ in range(3)]
    for k in range(3):
        stages[k][0] = gather_stage(k, 0)
    for s in range(2):
        for k in range(3):
            gather_wait(k, s, stages[k][s])
            stages[k][s + 1] = gather_stage(k, s + 1)

    for i in (2, 3):
        loads[i].wait()
        swaps[i].wait()
    for copy in gain_copies:
        copy.wait()
    for k in range(3):
        gather_wait(k, 2, stages[k][2])
        start, width = GATHER_LANES[k]

        def feed(block, _, start=start, width=width):
            bxh, by = block // 4, block % 4
            pieces = []
            sums = square[...]
            for t in range(start // 128, (start + width) // 128):
                part = xs[:, :, bxh, by, :, t * 128:(t + 1) * 128].reshape(256, 128).astype(F32)
                sums = sums + part * part
                scale = gains[2 * block + t // 4, t % 4:t % 4 + 1, :]
                pieces.append((part * scale).astype(BF16))
            square[...] = sums
            scaled = jnp.concatenate(pieces, axis=1)
            depth = pl.ds(pl.multiple_of(block * 1024 + start, 128), width)
            for acc, weight in (
                (acc_go, gate_own), (acc_gs, gate_sib), (acc_uo, up_own), (acc_us, up_sib)
            ):
                acc[...] += jnp.dot(scaled, weight[depth, :], preferred_element_type=F32)
            return 0

        lax.fori_loop(0, 8, feed, 0)

    norm = lax.rsqrt(jnp.sum(square[...], axis=1, keepdims=True) / D + 1e-05)
    for acc_g, acc_u, hid in ((acc_go, acc_uo, hid_own), (acc_gs, acc_us, hid_sib)):
        gate = acc_g[...] * norm
        hid[...] = (gate * jax.nn.sigmoid(gate) * (acc_u[...] * norm)).astype(BF16)

    lane_low = lax.broadcasted_iota(jnp.int32, (256, 128), 1) < 64
    odd = h % 2
    tiles = []
    for core in range(2):
        window = pl.ds(pl.multiple_of(core * 512 + (h // 2) * 128, 128), 128)
        tiles.append(xs[:, :, xh, y, :, window].reshape(256, 128).astype(F32))
    even_pack = jnp.where(lane_low, tiles[0], pltpu.roll(tiles[1], 64, 1))
    odd_pack = jnp.where(lane_low, pltpu.roll(tiles[0], 64, 1), tiles[1])
    packed = jnp.where(odd == 0, even_pack, odd_pack)
    res_z[:, c] = packed.astype(BF16).reshape(8, 32, 128)
    res_copy = pltpu.make_async_remote_copy(
        src_ref=res_z.at[:, c], dst_ref=res_z.at[:, c], send_sem=fin_s.at[0], recv_sem=fin_r.at[0],
        device_id=sibling, device_id_type=MESH,
    )
    res_copy.start()

    loads[4].wait()
    swaps[4].wait()

    def project(block, _):
        bxh, by = block // 4, block % 4
        col = pl.ds(pl.multiple_of(block * 1024, 1024), 1024)
        wide = jnp.dot(hid_own[...], down_own[:, col], preferred_element_type=F32)
        wide = wide + jnp.dot(hid_sib[...], down_sib[:, col], preferred_element_type=F32)
        for pair in range(4):
            low = wide[:, pair * 128:(pair + 1) * 128]
            high = wide[:, 512 + pair * 128:512 + (pair + 1) * 128]
            first = jnp.where(lane_low, low, pltpu.roll(high, 64, 1)).astype(BF16)
            second = jnp.where(lane_low, pltpu.roll(low, 64, 1), high).astype(BF16)
            ys[pair // 2, (pair % 2) * 2, bxh, by] = first
            ys[pair // 2, (pair % 2) * 2 + 1, bxh, by] = second
        return 0

    lax.fori_loop(0, 8, project, 0)

    def scatter_stage(k, s):
        order = SCATTER_ORDER[k]
        start, count = SCATTER_ROWS[k]
        axis = order[s]
        copies = []
        for d in range(1, 4):
            target = on_axis(axis, d)
            place = {a: (None if a in order[s + 1:] else target[a]) for a in "xyz"}
            copy = pltpu.make_async_remote_copy(
                src_ref=ys.at[(*block_index(place), pl.ds(start, count))],
                dst_ref=landing[k][s].at[d - 1],
                send_sem=sc_s.at[k, s, d - 1], recv_sem=sc_r.at[k, s, d - 1],
                device_id=at(target, c), device_id_type=MESH,
            )
            copy.start()
            copies.append(copy)
        return copies

    def scatter_sum(k, s, copies):
        order = SCATTER_ORDER[k]
        start, count = SCATTER_ROWS[k]
        for copy in copies:
            copy.wait_recv()
        kept = order[s + 1:]

        def add(block, _):
            place = dict(me)
            for i, a in enumerate(kept):
                place[a] = (block // 4**i) % 4
            spot = (*block_index(place), pl.ds(start, count))
            sums = ys[spot].astype(F32)
            for d in range(3):
                sums = sums + landing[k][s][(d, *kept_index(place, kept))].astype(F32)
            sums = sums.astype(BF16)
            if s < 2:
                ys[spot] = sums
            else:
                lay_z[start // 32:(start + count) // 32, c] = sums.reshape(count // 32, 32, 128)
            return 0

        if kept:
            lax.fori_loop(0, 4 ** len(kept), add, 0)
        else:
            add(0, 0)

    sums = [[None] * 3 for _ in range(3)]
    for k in range(3):
        sums[k][0] = scatter_stage(k, 0)
    for s in range(3):
        for k in range(3):
            scatter_sum(k, s, sums[k][s])
            if s < 2:
                sums[k][s + 1] = scatter_stage(k, s + 1)

    lay_copy = pltpu.make_async_remote_copy(
        src_ref=lay_z.at[:, c], dst_ref=lay_z.at[:, c], send_sem=fin_s.at[1], recv_sem=fin_r.at[1],
        device_id=sibling, device_id_type=MESH,
    )
    lay_copy.start()
    for k in range(3):
        for s in range(3):
            for copy in stages[k][s]:
                copy.wait_send()
            for copy in sums[k][s]:
                copy.wait_send()

    for copy, z_ref, out in ((res_copy, res_z, res_out), (lay_copy, lay_z, lay_out)):
        copy.wait_send()
        pltpu.make_async_remote_copy(
            src_ref=z_ref.at[:, 1 - c], dst_ref=z_ref.at[:, 1 - c],
            send_sem=fin_s.at[0], recv_sem=fin_r.at[0 if z_ref is res_z else 1],
            device_id=sibling, device_id_type=MESH,
        ).wait_recv()
        ordered = jnp.dot(perm[...], z_ref[...].reshape(512, 128), preferred_element_type=F32)
        ordered = jnp.where(c == 0, ordered, pltpu.roll(ordered, 64, 1))
        out[...] = ordered[:, 0:64].astype(BF16)


def layer(att, gain, slots, resid, out_w, gate_w, up_w, down_w):
    vmem = pl.BlockSpec(memory_space=pltpu.VMEM)
    hbm = pl.BlockSpec(memory_space=pl.ANY)
    dma = pltpu.SemaphoreType.DMA
    landing = []
    for k in range(3):
        for s in range(3):
            shape = (3, *kept_shape(SCATTER_ORDER[k][s + 1:]), SCATTER_ROWS[k][1], 128)
            landing.append(pltpu.VMEM(shape, BF16))
    return pl.pallas_call(
        layer_kernel,
        out_shape=[jax.ShapeDtypeStruct((512, 64), BF16)] * 2,
        in_specs=[vmem, vmem, vmem, hbm, hbm, hbm, hbm, hbm],
        out_specs=[vmem, vmem],
        scratch_shapes=[
            pltpu.VMEM((16, 8, 128), F32),
            pltpu.VMEM((8, 32, 1024), BF16),
            pltpu.VMEM((512, 512), BF16),
            pltpu.VMEM((512, 512), BF16),
            pltpu.VMEM((1024, 512), BF16),
            pltpu.VMEM((1024, 512), BF16),
            pltpu.VMEM((D, HID), BF16),
            pltpu.VMEM((D, HID), BF16),
            pltpu.VMEM((D, HID), BF16),
            pltpu.VMEM((D, HID), BF16),
            pltpu.VMEM((HID, D), BF16),
            pltpu.VMEM((HID, D), BF16),
            pltpu.VMEM((8, 32, 1024), BF16),
            pltpu.VMEM((7, 32, 1024), BF16),
            pltpu.VMEM((2, 4, 2, 4, 32, 1024), BF16),
            pltpu.VMEM((2, 4, 2, 4, 256, 128), BF16),
            pltpu.VMEM((256, HID), F32),
            pltpu.VMEM((256, HID), F32),
            pltpu.VMEM((256, HID), F32),
            pltpu.VMEM((256, HID), F32),
            pltpu.VMEM((256, 128), F32),
            pltpu.VMEM((512, 512), BF16),
            pltpu.VMEM((512, 128), F32),
            pltpu.VMEM((256, HID), BF16),
            pltpu.VMEM((256, HID), BF16),
            pltpu.VMEM((8, 2, 32, 128), BF16),
            pltpu.VMEM((8, 2, 32, 128), BF16),
            pltpu.VMEM((32, 1024), F32),
            *landing,
            dma((5,)),
            dma((5,)), dma((5,)),
            dma((7,)), dma((7,)),
            dma((15,)), dma((15,)),
            dma((7,)), dma((7,)),
            dma((3, 3, 3)), dma((3, 3, 3)),
            dma((3, 3, 3)), dma((3, 3, 3)),
            dma((2,)), dma((2,)),
        ],
        compiler_params=pltpu.CompilerParams(
            collective_id=0, has_side_effects=True, vmem_limit_bytes=56 * 2**20
        ),
        cost_estimate=pl.CostEstimate(flops=6 * 10**9, bytes_accessed=26 * 10**6, transcendentals=0),
        name="layer",
    )(att, gain, slots, resid, out_w, gate_w, up_w, down_w)


def per_device(
    query,
    new_key,
    new_value,
    key_cache,
    value_cache,
    lengths,
    slot_row,
    resid,
    out_weight,
    norm_gain,
    gate_weight,
    up_weight,
    down_weight,
):
    attended = attend_local(query, new_key, new_value, key_cache, value_cache, lengths)
    gain = jnp.pad(norm_gain.astype(F32).reshape(4, 128), ((0, 4), (0, 0)))
    slots = jnp.broadcast_to(slot_row[None, :], (8, 512))
    residual, output = layer(
        attended, gain, slots, resid, out_weight, gate_weight, up_weight, down_weight
    )
    return (residual, output)


def solution(mesh):
    placed = (
        P("grp", "head"),
        P("grp", "head"),
        P("grp", "head"),
        P("grp", "head", None, None),
        P("grp", "head", None, None),
        P("grp"),
        P(),
        P(None, "grp"),
        P("head", "grp"),
        P("grp"),
        P(None, ("grp", "head")),
        P(None, ("grp", "head")),
        P(("grp", "head"), None),
    )
    return jax.shard_map(
        per_device,
        mesh=mesh,
        in_specs=placed,
        out_specs=(P(None, ("grp", "head")), P(None, ("grp", "head"))),
        check_vma=False,
    )
```

time: 957 us -> 132 us (0.14); the launches traced: 941 us -> 132 us
  waiting for transfers between devices: 835 us -> 0 us
  Pallas kernels: 0 us -> 101 us
  blocking collectives: 38.3 us -> 0 us
  matrix products: 34.1 us -> 7.18 us
  between operations: 14 us -> 0.68 us
    reduce_scatter x1 -> x0, waiting for transfers between devices: 647 us -> none  [layer_rows(): lax.psum_scatter(ffn_terms, ('grp', 'head'), scatter_dimension=1, tiled=T...]
    all_gather x2 -> x0, waiting for transfers between devices: 123 us -> none  [the longest x1 74.3 us: layer_rows(): block_cols = lax.all_gather(normed, 'grp', axis=1, tiled=True)]
    pallas_call x0 -> x1, Pallas kernels: none -> 101 us  [layer(): pl.pallas_call(layer_kernel, out_shape=[jax.ShapeDtypeStruct((512, 64), B...]
    psum x1 -> x0, waiting for transfers between devices: 65 us -> none  [layer_rows(): summed = lax.psum(partial_proj, 'head')]
    psum x1 -> x0, blocking collectives: 38.3 us -> none  [layer_rows(): sum_squares = lax.psum(jnp.sum(stream * stream, axis=1), 'grp')]
    dot_general x3 -> x0, matrix products: 26.3 us -> none  [the longest x1 16.2 us: layer_rows(): ffn_terms = jnp.dot(hidden, down_weight, preferred_element_type=jnp.float32)]
    unnamed x14 -> x8, local copies, waits for them, and re-layouts: 3.29 us -> 14.7 us
  transfers between devices with their start and end apart: 4 -> 0, of which waited for: 4 -> 0; matrix products, arithmetic and copies ran while one was open for 1% -> 0% of each run, Pallas kernels for 0% -> 0%
where the time goes in v1:
time: 132 us
  Pallas kernels  101 us (77%)
  local copies, waits for them, and re-layouts  19.2 us (15%)
  matrix products  7.18 us (5%)
  other arithmetic  3.6 us (3%)
    pallas_call x1, Pallas kernels, layer(): pl.pallas_call(layer_kernel, out_shape=[jax.ShapeDtypeStruct((512, 64), B...  101 us
    unnamed x8, local copies, waits for them, and re-layouts  14.7 us
    dot_general x1, matrix products, attend_local(): jnp.einsum('rjqd,rjpd->rjqp', query_heads, key_cache, preferred_element_t...  5.74 us
    pallas_call x2, local copies, waits for them, and re-layouts, layer(): pl.pallas_call(layer_kernel, out_shape=[jax.ShapeDtypeStruct((512, 64), B...  3.24 us

profile of v1, /device:TPU:1, one launch (start us, length us, event | category | flops | bytes accessed | tf_op | source)
XLA Modules:
  0.0 131.9 jit_solution(16618234884706649455)
XLA Ops:
  0.6 0.0 copy-start
  0.6 0.0 copy-start.1
  0.7 0.7 copy-done
  1.3 1.6 %pad_convert_fusion.gain = f32[8,128]{1,0:T(8,128)} fusion(bf16[4,128]{1,0:T(4,128)(2,1)} %bitcast.36), kind=kLoop, calls=%fused_computation.24 | loop fusion | flops 1024 | bytes 5120 | tf_op jit(solution)/shard_map/jit(_pad)/pad | solution.py:506
  2.9 0.9 convert_element_type.27
  3.8 1.3 broadcast_in_dim.33.slots
  5.0 0.7 iota_compare_fusion
  5.8 0.9 copy.21
  6.6 0.1 fusion.21
  6.8 5.7 %fusion.26 = (f32[32,8]{1,0:T(8,128)S(1)}, f32[32,8,1024]{2,1,0:T(8,128)S(1)}) fusion(bf16[32,8,128]{2,1,0:T(8,128)(2,1)S(1)} %bitcast.31, bf16[32,1,1024,128]{3,2,1,0:T(8,128)(2,1)} %param.16, pred[32,1024]{1,0:T(8,128)(4,1)S(1)} %iota_compare_fusion), kind=kOutput, calls=%fused_computation.26 | convolution fusion | flops 67895040 | bytes 9536512 | tf_op jit(solution)/shard_map/rjqd,rjpd->rjqp/dot_general | solution.py:28
  12.5 0.4 fusion.16
  13.0 0.0 copy-done.1
  13.0 1.3 fusion.13
  14.3 0.7 copy.26
  14.9 6.3 %copy.15.gate_w = bf16[8192,224]{1,0:T(8,128)(2,1)} copy(bf16[8192,224]{0,1:T(8,128)(2,1)} %param.23) | data formatting | bytes 7340032 | tf_op args[10]
  21.2 6.2 %copy.16.up_w = bf16[8192,224]{1,0:T(8,128)(2,1)} copy(bf16[8192,224]{0,1:T(8,128)(2,1)} %param.24) | data formatting | bytes 7340032 | tf_op args[11]
  27.4 101.2 %layer.1 = (bf16[512,64]{1,0:T(8,128)(2,1)}, bf16[512,64]{1,0:T(8,128)(2,1)}) custom-call(bf16[32,1024]{1,0:T(8,128)(2,1)} %bitcast.35, f32[8,128]{1,0:T(8,128)} %pad_convert_fusion.gain, s32[8,512]{1,0:T(8,128)} %broadcast_in_dim.33.slots, bf16[512,512]{1,0:T(8,128)(2,1)} %resid.1, bf16[1024,512]{1,0:T(8,128)(2,1)} %out_w.1, ...), custom_call_target="tpu_custom_call" | custom-call | flops 6000000000 | bytes 26000000 | tf_op jit(solution)/shard_map/layer/pallas_call | solution.py:438
  128.7 1.6 %copy.17 = bf16[512,64]{0,1:T(8,128)(2,1)} copy(bf16[512,64]{1,0:T(8,128)(2,1)} %get-tuple-element.2) | data formatting | bytes 131072 | tf_op jit(solution)/shard_map/layer/pallas_call | solution.py:438
  130.3 1.6 %copy.18 = bf16[512,64]{0,1:T(8,128)(2,1)} copy(bf16[512,64]{1,0:T(8,128)(2,1)} %get-tuple-element.3) | data formatting | bytes 131072 | tf_op jit(solution)/shard_map/layer/pallas_call | solution.py:438
  (2 shorter events, 0.0 us)
Async XLA Ops:
  0.6 0.7 copy-start
  0.6 12.3 %copy-start.1 = (bf16[32,1,1024,128]{3,2,1,0:T(8,128)(2,1)S(1)}, bf16[32,1,1024,128]{3,2,1,0:T(8,128)(2,1)}, u32[]{:S(2)}) copy-start(bf16[32,1,1024,128]{3,2,1,0:T(8,128)(2,1)} %param.17) | copy-start | bytes 25165828

commit v2 on v1

v2 whole, which is shorter than its diff:
```python
import jax
import jax.numpy as jnp
from jax import lax
from jax.experimental import pallas as pl
from jax.experimental.pallas import tpu as pltpu
from jax.sharding import PartitionSpec as P

D = 8192
HD = 128
PER_KV = 8
CTX = 1024
SLOTS = 32
HID = 224
RING = 8
UNROLL = 4
MESH = pl.DeviceIdType.MESH
BF16 = jnp.bfloat16
F32 = jnp.float32
NT = (((1,), (1,)), ((), ()))

GATHER_LANES = ((0, 384), (384, 384), (768, 256))
GATHER_ORDER = ("zxy", "yzx", "xyz")
SCATTER_ROWS = ((0, 96), (96, 96), (192, 64))
SCATTER_ORDER = ("yzx", "zxy", "xyz")
BESIDE = (0, -1, 1, 2)


def device_at(x, y, z, c):
    return ((x // 2) * 8 + y * 2 + c, (x % 2) * 4 + z)


def block_index(where):
    x, y, z = where["x"], where["y"], where["z"]
    if x is None:
        xl, xh = slice(None), slice(None)
    else:
        xl, xh = x % 2, x // 2
    return (xl, slice(None) if z is None else z, xh, slice(None) if y is None else y)


def kept_index(where, kept):
    index = ()
    if "x" in kept:
        index += (where["x"] % 2,)
    if "z" in kept:
        index += (where["z"],)
    if "x" in kept:
        index += (where["x"] // 2,)
    if "y" in kept:
        index += (where["y"],)
    return index


def kept_shape(kept):
    shape = ()
    if "x" in kept:
        shape += (2,)
    if "z" in kept:
        shape += (4,)
    if "x" in kept:
        shape += (2,)
    if "y" in kept:
        shape += (4,)
    return shape


def layer_kernel(
    query, new_key, new_value, lengths, gain, slots, keys, values, resid, out_w, gate_w, up_w, down_w,
    res_out, lay_out,
    key_ring, value_ring, heads, mixed, new_key_f, new_value_f,
    gain_own, gains, got_att, resid_own, resid_sib, ow_own, ow_sib,
    gate_up, down_all,
    proj, proj_got, xs, ys, acc, square,
    perm, slot_col, hidden, res_z, lay_z, res_rows,
    *rest,
):
    landing = [[rest[k * 3 + s] for s in range(3)] for k in range(3)]
    transit = [[rest[9 + k * 3 + s] for s in range(3)] for k in range(3)]
    (kv_sem, load_sem, swap_s, swap_r, att_s, att_r, gain_s, gain_r, proj_s, proj_r,
     ga_s, ga_r, sc_s, sc_r, fin_s, fin_r) = rest[18:]

    g = lax.axis_index("grp")
    h = lax.axis_index("head")
    xh, y, c = g // 8, (g // 2) % 4, g % 2
    xl, z = h // 4, h % 4
    me = {"x": xh * 2 + xl, "y": y, "z": z}

    def on_axis(axis, step):
        place = dict(me)
        place[axis] = (me[axis] + step + 4) % 4
        return place

    def at(place, core):
        return device_at(place["x"], place["y"], place["z"], core)

    sibling = at(me, 1 - c)
    barrier = pltpu.get_barrier_semaphore()
    partners = []
    for i in range(1, 16):
        partners.append(((g + i) % 16, h))
    for i in range(1, 8):
        partners.append((g, (h + i) % 8))
    partners.append(((g + 8) % 16, (h + 4) % 8))
    for partner in partners:
        pl.semaphore_signal(barrier, inc=1, device_id=partner, device_id_type=MESH)

    def cache_copies(row, ring):
        return (
            pltpu.make_async_copy(keys.at[row, 0], key_ring.at[ring], kv_sem.at[0, ring]),
            pltpu.make_async_copy(values.at[row, 0], value_ring.at[ring], kv_sem.at[1, ring]),
        )

    for row in range(RING):
        for copy in cache_copies(row, row):
            copy.start()
    new_key_f[...] = new_key[...].astype(F32)
    new_value_f[...] = new_value[...].astype(F32)
    for j in range(PER_KV):
        heads[:, j, :] = query[:, j * HD:(j + 1) * HD].astype(F32)
    for t in range(4):
        gain_own[t:t + 1, :] = gain[:, t * 128:(t + 1) * 128].astype(F32)
    gain_own[4:8, :] = jnp.zeros((4, 128), F32)
    pl.semaphore_wait(barrier, len(partners))

    swaps = []
    for i, (src, dst) in enumerate(
        ((out_w, ow_sib), (resid, resid_sib), (gate_w, gate_up.at[pl.ds(HID, HID)]),
         (up_w, gate_up.at[pl.ds(3 * HID, HID)]), (down_w, down_all.at[pl.ds(HID, HID)]))
    ):
        copy = pltpu.make_async_remote_copy(
            src_ref=src, dst_ref=dst, send_sem=swap_s.at[i], recv_sem=swap_r.at[i],
            device_id=sibling, device_id_type=MESH,
        )
        copy.start()
        swaps.append(copy)
    gain_copies = []
    for i in range(1, 16):
        copy = pltpu.make_async_remote_copy(
            src_ref=gain_own,
            dst_ref=gains.at[g],
            send_sem=gain_s.at[i - 1],
            recv_sem=gain_r.at[i - 1],
            device_id=((g + i) % 16, h),
            device_id_type=MESH,
        )
        copy.start()
        gain_copies.append(copy)
    gains[g] = gain_own[...]

    spot_lane = lax.broadcasted_iota(jnp.int32, (PER_KV, CTX), 1)

    def attend(step, _):
        for u in range(UNROLL):
            row = step * UNROLL + u
            ring = row % RING
            for copy in cache_copies(row, ring):
                copy.wait()
        for u in range(UNROLL):
            row = step * UNROLL + u
            ring = row % RING
            head = heads[row]
            scores = lax.dot_general(
                head.astype(BF16), key_ring[ring], NT, preferred_element_type=F32
            ) * HD ** (-0.5)
            own = jnp.sum(head * new_key_f[pl.ds(row, 1), :], axis=1, keepdims=True) * HD ** (-0.5)
            live = spot_lane < lengths[row]
            scores = jnp.where(live, scores, -1e30)
            top = jnp.maximum(jnp.max(scores, axis=1, keepdims=True), own)
            weights = jnp.where(live, jnp.exp(scores - top), 0.0)
            own = jnp.exp(own - top)
            share = 1.0 / (jnp.sum(weights, axis=1, keepdims=True) + own)
            weights = (weights * share).astype(BF16)
            own = (own * share).astype(BF16).astype(F32)
            result = jnp.dot(weights, value_ring[ring], preferred_element_type=F32)
            mixed[row] = result + own * new_value_f[pl.ds(row, 1), :]
        for u in range(UNROLL):
            row = step * UNROLL + u
            ring = row % RING

            @pl.when(row + RING < SLOTS)
            def _():
                for copy in cache_copies(row + RING, ring):
                    copy.start()
        return 0

    att_copies = []
    half = SLOTS // 2
    for part in range(2):
        steps = half // UNROLL
        lax.fori_loop(part * steps, (part + 1) * steps, attend, 0)
        rows = pl.ds(part * half, half)
        for j in range(PER_KV):
            got_att[xh * 4 + y, rows, j * HD:(j + 1) * HD] = mixed[rows, j, :].astype(BF16)
        for i in (6, 5, 4, 2, 7, 3, 1):
            xy = ((xh + i // 4) % 2) * 4 + (y + i) % 4
            copy = pltpu.make_async_remote_copy(
                src_ref=got_att.at[xh * 4 + y, rows],
                dst_ref=got_att.at[xh * 4 + y, rows],
                send_sem=att_s.at[part, i - 1],
                recv_sem=att_r.at[part, i - 1],
                device_id=((xy // 4) * 8 + (xy % 4) * 2 + c, h),
                device_id_type=MESH,
            )
            copy.start()
            att_copies.append((i, copy))
    loads = []
    for i, (src, dst) in enumerate(
        ((out_w, ow_own), (resid, resid_own), (gate_w, gate_up.at[pl.ds(0, HID)]),
         (up_w, gate_up.at[pl.ds(2 * HID, HID)]), (down_w, down_all.at[pl.ds(0, HID)]))
    ):
        copy = pltpu.make_async_copy(src, dst, load_sem.at[i])
        copy.start()
        loads.append(copy)

    slot_line = slots[...]
    for t in range(4):
        tile = jnp.broadcast_to(slot_line[:, t * 128:(t + 1) * 128].astype(F32), (128, 128))
        slot_col[t * 128:(t + 1) * 128, :] = tile.T
        batch = lax.broadcasted_iota(jnp.int32, (128, 512), 0) + t * 128
        perm[t * 128:(t + 1) * 128, :] = jnp.where(batch == slot_line, 1.0, 0.0).astype(BF16)
    square[...] = jnp.zeros_like(square)
    acc[...] = jnp.zeros_like(acc)

    loads[1].wait()
    swaps[1].wait()
    my_slots = slot_col[pl.ds(pl.multiple_of((2 * h + c) * 32, 32), 32), :]
    lane = lax.broadcasted_iota(jnp.int32, (32, 128), 1).astype(F32)
    pick = jnp.concatenate(
        [jnp.where(my_slots == lane + 128.0 * t, 1.0, 0.0).astype(BF16) for t in range(4)], axis=1
    )

    @pl.when(c == 0)
    def _():
        res_rows[:, 0:512] = jnp.dot(pick, resid_own[...], preferred_element_type=F32)
        res_rows[:, 512:1024] = jnp.dot(pick, resid_sib[...], preferred_element_type=F32)

    @pl.when(c == 1)
    def _():
        res_rows[:, 0:512] = jnp.dot(pick, resid_sib[...], preferred_element_type=F32)
        res_rows[:, 512:1024] = jnp.dot(pick, resid_own[...], preferred_element_type=F32)

    loads[0].wait()
    swaps[0].wait()
    for side in range(2):
        for i, copy in att_copies:
            if (i < 4) == (side == 0):
                copy.wait()
        xx = (xh + side) % 2
        part = got_att[pl.ds(xx * 4, 4)].reshape(128, 1024)
        own_part = jnp.dot(part, ow_own[...], preferred_element_type=F32).astype(BF16)
        sib_part = jnp.dot(part, ow_sib[...], preferred_element_type=F32).astype(BF16)
        proj[pl.ds(xx * 4, 4), :, pl.ds(pl.multiple_of(c * 512, 512), 512)] = own_part.reshape(4, 32, 512)
        proj[pl.ds(xx * 4, 4), :, pl.ds(pl.multiple_of((1 - c) * 512, 512), 512)] = sib_part.reshape(
            4, 32, 512
        )
        for k in range(3):
            lanes = pl.ds(*GATHER_LANES[k])
            for j in range(4):
                head = xx * 4 + (z + 2 + j) % 4

                @pl.when(head != h)
                def _():
                    pltpu.make_async_remote_copy(
                        src_ref=proj.at[head, :, lanes],
                        dst_ref=proj_got.at[h, :, lanes],
                        send_sem=proj_s.at[k, head],
                        recv_sem=proj_r.at[k, h],
                        device_id=(g, head),
                        device_id_type=MESH,
                    ).start()

    def proj_copy(k, head):
        lanes = pl.ds(*GATHER_LANES[k])
        return pltpu.make_async_remote_copy(
            src_ref=proj.at[head, :, lanes],
            dst_ref=proj_got.at[head, :, lanes],
            send_sem=proj_s.at[k, head],
            recv_sem=proj_r.at[k, head],
            device_id=(g, head),
            device_id_type=MESH,
        )

    gathers = {}

    def gather_spot(k, s, q, shift):
        order = GATHER_ORDER[k]
        place = dict(me)
        for a in order[:s]:
            place[a] = None
        if s == 2:
            place[order[1]] = (me[order[1]] + BESIDE[q] + 4) % 4
        place[order[s]] = (me[order[s]] + shift + 4) % 4
        return place

    def gather_copy(k, s, q, which):
        shift, rows, step = (
            (0, pl.ds(0, 32), 1), (0, pl.ds(0, 32), -1), (-1, pl.ds(0, 16), 1), (1, pl.ds(16, 16), -1)
        )[which]
        region = xs.at[(*block_index(gather_spot(k, s, q, shift)), rows, pl.ds(*GATHER_LANES[k]))]
        index = 4 * (s + q) + which
        copy = pltpu.make_async_remote_copy(
            src_ref=region, dst_ref=region, send_sem=ga_s.at[k, index], recv_sem=ga_r.at[k, index],
            device_id=at(on_axis(GATHER_ORDER[k][s], step), c), device_id_type=MESH,
        )
        copy.start()
        gathers[k, s, q, which] = copy

    def direct(k, s, q):
        gather_copy(k, s, q, 0)
        gather_copy(k, s, q, 1)

    def forward(k, s, q):
        gathers[k, s, q, 0].wait_recv()
        gather_copy(k, s, q, 2)
        gathers[k, s, q, 1].wait_recv()
        gather_copy(k, s, q, 3)

    def finish(k, s, q):
        gathers[k, s, q, 2].wait_recv()
        gathers[k, s, q, 3].wait_recv()

    mine = block_index(me)
    for k in range(3):
        lanes = pl.ds(*GATHER_LANES[k])
        total = res_rows[:, lanes] + proj[h, :, lanes].astype(F32)
        for i in range(1, 8):
            head = (h + i) % 8
            proj_copy(k, head).wait_recv()
            total = total + proj_got[head, :, lanes].astype(F32)
        xs[(*mine, slice(None), lanes)] = total.astype(BF16)
        direct(k, 0, 0)
    for k in range(3):
        forward(k, 0, 0)
    for k in range(3):
        finish(k, 0, 0)
        direct(k, 1, 0)
        direct(k, 2, 0)
    for k in range(3):
        forward(k, 1, 0)
        direct(k, 2, 1)
        direct(k, 2, 2)
    for k in range(3):
        finish(k, 1, 0)
        direct(k, 2, 3)

    def feed(k, blocks):
        start, width = GATHER_LANES[k]
        total = None
        sums = square[...]
        for bxh, by in blocks:
            block = bxh * 4 + by
            pieces = []
            for t in range(start // 128, (start + width) // 128):
                part = xs[:, :, bxh, by, :, t * 128:(t + 1) * 128].reshape(256, 128).astype(F32)
                sums = sums + part * part
                scale = gains[2 * block + t // 4, t % 4:t % 4 + 1, :]
                pieces.append((part * scale).astype(BF16))
            scaled = jnp.concatenate(pieces, axis=1)
            depth = pl.ds(pl.multiple_of(block * 1024 + start, 128), width)
            term = lax.dot_general(gate_up[:, depth], scaled, NT, preferred_element_type=F32)
            total = term if total is None else total + term
        square[...] = sums
        acc[...] += total

    def feed_y(k, by):
        feed(k, ((0, by), (1, by)))

    def feed_x(k, bxh):
        def pair(i, _):
            feed(k, ((bxh, 2 * i), (bxh, 2 * i + 1)))
            return 0

        lax.fori_loop(0, 2, pair, 0)

    def feed_all(k):
        def pair(i, _):
            feed(k, ((0, i), (1, i)))
            return 0

        lax.fori_loop(0, 4, pair, 0)

    for copy in gain_copies:
        copy.wait()
    for i in (2, 3):
        loads[i].wait()
        swaps[i].wait()
    feed_y(0, y)
    for q in range(4):
        for k in (2, 0, 1):
            forward(k, 2, q)
    feed_y(0, (y + 1) % 4)
    feed_y(0, (y + 3) % 4)
    feed_x(1, xh)
    for q in range(4):
        finish(2, 2, q)
    feed_all(2)
    for q in range(4):
        finish(0, 2, q)
    feed_y(0, (y + 2) % 4)
    for q in range(4):
        finish(1, 2, q)
    feed_x(1, 1 - xh)

    norm = lax.rsqrt(jnp.sum(square[...].T, axis=0, keepdims=True) / D + 1e-05)
    gate = acc[0:2 * HID, :] * norm
    up = acc[2 * HID:4 * HID, :] * norm
    hidden[...] = (gate * jax.nn.sigmoid(gate) * up).T.astype(BF16)

    lane_low = lax.broadcasted_iota(jnp.int32, (256, 128), 1) < 64
    odd = h % 2
    tiles = []
    for core in range(2):
        window = pl.ds(pl.multiple_of(core * 512 + (h // 2) * 128, 128), 128)
        tiles.append(xs[:, :, xh, y, :, window].reshape(256, 128).astype(F32))
    even_pack = jnp.where(lane_low, tiles[0], pltpu.roll(tiles[1], 64, 1))
    odd_pack = jnp.where(lane_low, pltpu.roll(tiles[0], 64, 1), tiles[1])
    packed = jnp.where(odd == 0, even_pack, odd_pack)
    res_z[:, c] = packed.astype(BF16).reshape(8, 32, 128)
    res_copy = pltpu.make_async_remote_copy(
        src_ref=res_z.at[:, c], dst_ref=res_z.at[:, c], send_sem=fin_s.at[0], recv_sem=fin_r.at[0],
        device_id=sibling, device_id_type=MESH,
    )
    res_copy.start()

    loads[4].wait()
    swaps[4].wait()

    def project(block, _):
        bxh, by = block // 4, block % 4
        col = pl.ds(pl.multiple_of(block * 1024, 1024), 1024)
        wide = jnp.dot(hidden[...], down_all[:, col], preferred_element_type=F32)
        for pair in range(4):
            low = wide[:, pair * 128:(pair + 1) * 128]
            high = wide[:, 512 + pair * 128:512 + (pair + 1) * 128]
            first = jnp.where(lane_low, low, pltpu.roll(high, 64, 1)).astype(BF16)
            second = jnp.where(lane_low, pltpu.roll(low, 64, 1), high).astype(BF16)
            ys[pair // 2, (pair % 2) * 2, bxh, by] = first
            ys[pair // 2, (pair % 2) * 2 + 1, bxh, by] = second
        return 0

    lax.fori_loop(0, 8, project, 0)

    scatters = {}

    def halves(k):
        start, count = SCATTER_ROWS[k]
        return ((start, count // 2), (start + count // 2, count // 2))

    def scatter_place(k, s, shift):
        order = SCATTER_ORDER[k]
        place = dict(me)
        place[order[s]] = (me[order[s]] + shift + 4) % 4
        for a in order[s + 1:]:
            place[a] = None
        return place

    def scatter_copy(k, s, which):
        target, part, step = ((2, 0, 1), (2, 1, -1), (1, 1, 1), (-1, 0, -1), (1, 0, 1), (-1, 1, -1))[which]
        start, count = halves(k)[part]
        if which < 2:
            dst = transit[k][s].at[which]
        else:
            side = 0 if step == 1 else 1
            everything = (slice(None),) * len(kept_shape(SCATTER_ORDER[k][s + 1:]))
            dst = landing[k][s].at[(side, *everything, pl.ds(start - SCATTER_ROWS[k][0], count))]
        copy = pltpu.make_async_remote_copy(
            src_ref=ys.at[(*block_index(scatter_place(k, s, target)), pl.ds(start, count))],
            dst_ref=dst, send_sem=sc_s.at[k, s, which], recv_sem=sc_r.at[k, s, which],
            device_id=at(on_axis(SCATTER_ORDER[k][s], step), c), device_id_type=MESH,
        )
        copy.start()
        scatters[k, s, which] = copy

    def each_block(k, s, shift, body):
        kept = SCATTER_ORDER[k][s + 1:]

        def one(block, _):
            place = scatter_place(k, s, shift)
            for i, a in enumerate(kept):
                place[a] = (block // 4**i) % 4
            body(block_index(place), kept_index(place, kept))
            return 0

        if kept:
            lax.fori_loop(0, 4 ** len(kept), one, 0)
        else:
            one(0, 0)

    def scatter_begin(k, s):
        for which in range(4):
            scatter_copy(k, s, which)

    def scatter_pass(k, s):
        for which, shift in ((0, 1), (1, -1)):
            scatters[k, s, which].wait_recv()
            rows = pl.ds(*halves(k)[which])

            def add(spot, kept_spot, which=which, rows=rows):
                both = ys[(*spot, rows)].astype(F32) + transit[k][s][(which, *kept_spot)].astype(F32)
                ys[(*spot, rows)] = both.astype(BF16)

            each_block(k, s, shift, add)
            scatter_copy(k, s, 4 + which)

    def scatter_end(k, s):
        for which in range(2, 6):
            scatters[k, s, which].wait_recv()
        start, count = SCATTER_ROWS[k]
        rows = pl.ds(start, count)

        def add(spot, kept_spot):
            sums = ys[(*spot, rows)].astype(F32)
            for side in range(2):
                sums = sums + landing[k][s][(side, *kept_spot)].astype(F32)
            sums = sums.astype(BF16)
            if s < 2:
                ys[(*spot, rows)] = sums
            else:
                lay_z[start // 32:(start + count) // 32, c] = sums.reshape(count // 32, 32, 128)

        each_block(k, s, 0, add)

    for k in range(3):
        scatter_begin(k, 0)
    for s in range(3):
        for k in range(3):
            scatter_pass(k, s)
        for k in range(3):
            scatter_end(k, s)
            if s < 2:
                scatter_begin(k, s + 1)

    lay_copy = pltpu.make_async_remote_copy(
        src_ref=lay_z.at[:, c], dst_ref=lay_z.at[:, c], send_sem=fin_s.at[1], recv_sem=fin_r.at[1],
        device_id=sibling, device_id_type=MESH,
    )
    lay_copy.start()
    for k in range(3):
        for i in range(1, 8):
            proj_copy(k, (h + i) % 8).wait_send()
    for copy in gathers.values():
        copy.wait_send()
    for copy in scatters.values():
        copy.wait_send()

    for i, (copy, z_ref, out) in enumerate(((res_copy, res_z, res_out), (lay_copy, lay_z, lay_out))):
        copy.wait_send()
        pltpu.make_async_remote_copy(
            src_ref=z_ref.at[:, 1 - c], dst_ref=z_ref.at[:, 1 - c],
            send_sem=fin_s.at[i], recv_sem=fin_r.at[i],
            device_id=sibling, device_id_type=MESH,
        ).wait_recv()
        ordered = jnp.dot(perm[...], z_ref[...].reshape(512, 128), preferred_element_type=F32)
        ordered = jnp.where(c == 0, ordered, pltpu.roll(ordered, 64, 1))
        out[...] = ordered.T[0:64, :].astype(BF16)


def layer(query, new_key, new_value, lengths, gain, slots, *hbm_args):
    vmem = pl.BlockSpec(memory_space=pltpu.VMEM)
    smem = pl.BlockSpec(memory_space=pltpu.SMEM)
    hbm = pl.BlockSpec(memory_space=pl.ANY)
    dma = pltpu.SemaphoreType.DMA
    landing, transit = [], []
    for k in range(3):
        for s in range(3):
            kept, count = kept_shape(SCATTER_ORDER[k][s + 1:]), SCATTER_ROWS[k][1]
            landing.append(pltpu.VMEM((2, *kept, count, 128), BF16))
            transit.append(pltpu.VMEM((2, *kept, count // 2, 128), BF16))
    return pl.pallas_call(
        layer_kernel,
        out_shape=[jax.ShapeDtypeStruct((64, 512), BF16)] * 2,
        in_specs=[vmem, vmem, vmem, smem, vmem, vmem] + [hbm] * len(hbm_args),
        out_specs=[vmem, vmem],
        scratch_shapes=[
            pltpu.VMEM((RING, CTX, HD), BF16),
            pltpu.VMEM((RING, CTX, HD), BF16),
            pltpu.VMEM((SLOTS, PER_KV, HD), F32),
            pltpu.VMEM((SLOTS, PER_KV, HD), F32),
            pltpu.VMEM((SLOTS, HD), F32),
            pltpu.VMEM((SLOTS, HD), F32),
            pltpu.VMEM((8, 128), F32),
            pltpu.VMEM((16, 8, 128), F32),
            pltpu.VMEM((8, 32, 1024), BF16),
            pltpu.VMEM((512, 512), BF16),
            pltpu.VMEM((512, 512), BF16),
            pltpu.VMEM((1024, 512), BF16),
            pltpu.VMEM((1024, 512), BF16),
            pltpu.VMEM((4 * HID, D), BF16),
            pltpu.VMEM((2 * HID, D), BF16),
            pltpu.VMEM((8, 32, 1024), BF16),
            pltpu.VMEM((8, 32, 1024), BF16),
            pltpu.VMEM((2, 4, 2, 4, 32, 1024), BF16),
            pltpu.VMEM((2, 4, 2, 4, 256, 128), BF16),
            pltpu.VMEM((4 * HID, 256), F32),
            pltpu.VMEM((256, 128), F32),
            pltpu.VMEM((512, 512), BF16),
            pltpu.VMEM((512, 128), F32),
            pltpu.VMEM((256, 2 * HID), BF16),
            pltpu.VMEM((8, 2, 32, 128), BF16),
            pltpu.VMEM((8, 2, 32, 128), BF16),
            pltpu.VMEM((32, 1024), F32),
            *landing,
            *transit,
            dma((2, RING)),
            dma((5,)),
            dma((5,)), dma((5,)),
            dma((2, 7)), dma((2, 7)),
            dma((15,)), dma((15,)),
            dma((3, 8)), dma((3, 8)),
            dma((3, 24)), dma((3, 24)),
            dma((3, 3, 6)), dma((3, 3, 6)),
            dma((2,)), dma((2,)),
        ],
        compiler_params=pltpu.CompilerParams(
            collective_id=0, has_side_effects=True, vmem_limit_bytes=58 * 2**20
        ),
        cost_estimate=pl.CostEstimate(flops=6 * 10**9, bytes_accessed=42 * 10**6, transcendentals=0),
        name="layer",
    )(query, new_key, new_value, lengths, gain, slots, *hbm_args)


def per_device(
    query,
    new_key,
    new_value,
    key_cache,
    value_cache,
    lengths,
    slot_row,
    resid,
    out_weight,
    norm_gain,
    gate_weight,
    up_weight,
    down_weight,
):
    residual, output = layer(
        query, new_key, new_value, lengths, norm_gain[None, :], slot_row[None, :],
        key_cache, value_cache, resid, out_weight, gate_weight.T, up_weight.T, down_weight,
    )
    return (residual.T, output.T)


def solution(mesh):
    placed = (
        P("grp", "head"),
        P("grp", "head"),
        P("grp", "head"),
        P("grp", "head", None, None),
        P("grp", "head", None, None),
        P("grp"),
        P(),
        P(None, "grp"),
        P("head", "grp"),
        P("grp"),
        P(None, ("grp", "head")),
        P(None, ("grp", "head")),
        P(("grp", "head"), None),
    )
    return jax.shard_map(
        per_device,
        mesh=mesh,
        in_specs=placed,
        out_specs=(P(None, ("grp", "head")), P(None, ("grp", "head"))),
        check_vma=False,
    )
```

time: 132 us -> 108 us (0.82)
  local copies, waits for them, and re-layouts: 19.2 us -> 4.21 us
  matrix products: 7.18 us -> 0 us
  other arithmetic: 3.6 us -> 0 us
  Pallas kernels: 101 us -> 103 us
    unnamed x8 -> x2, local copies, waits for them, and re-layouts: 14.7 us -> 2.95 us
    dot_general x3 -> x0, matrix products: 7.18 us -> none  [the longest x1 5.74 us: attend_local(): jnp.einsum('rjqd,rjpd->rjqp', query_heads, key_cache, preferred_element_t...]
    pallas_call x2 -> x0, local copies, waits for them, and re-layouts: 3.24 us -> none  [layer(): pl.pallas_call(layer_kernel, out_shape=[jax.ShapeDtypeStruct((512, 64), B...]
    pallas_call x1, Pallas kernels: 101 us -> 103 us  [layer(): pl.pallas_call(layer_kernel, out_shape=[jax.ShapeDtypeStruct((64, 512), B...]
    pad x1 -> x0, other arithmetic: 1.56 us -> none  [per_device(): gain = jnp.pad(norm_gain.astype(F32).reshape(4, 128), ((0, 4), (0, 0)))]
where the time goes in v2:
time: 108 us
  Pallas kernels  103 us (95%)
  local copies, waits for them, and re-layouts  4.21 us (4%)
    pallas_call x1, Pallas kernels, layer(): pl.pallas_call(layer_kernel, out_shape=[jax.ShapeDtypeStruct((64, 512), B...  103 us
    unnamed x2, local copies, waits for them, and re-layouts  2.95 us

profile of v2, /device:TPU:1, one launch (start us, length us, event | category | flops | bytes accessed | tf_op | source)
XLA Modules:
  0.0 107.9 jit_solution(331738535226135098)
XLA Ops:
  0.6 1.3 %broadcast_in_dim.6.gain = bf16[1,512]{1,0:T(2,128)(2,1)} reshape(bf16[512]{0:T(512)(128)(2,1)} %param.22) | data formatting | bytes 2048 | tf_op jit(solution)/shard_map/broadcast_in_dim | solution.py:638
  1.9 103.0 %layer.1 = (bf16[64,512]{1,0:T(8,128)(2,1)}, bf16[64,512]{1,0:T(8,128)(2,1)}) custom-call(bf16[32,1024]{1,0:T(8,128)(2,1)} %query.1, bf16[32,128]{1,0:T(8,128)(2,1)} %new_key.1, bf16[32,128]{1,0:T(8,128)(2,1)} %new_value.1, s32[32]{0:T(128)} %lengths.1, bf16[1,512]{1,0:T(2,128)(2,1)} %broadcast_in_dim.6.gain, s32[1,512]{1,0:T(1,128)} %bitcast.9, ...), custom_call_target="tpu_custom_call" | custom-call | flops 6000000000 | bytes 42000000 | tf_op jit(solution)/shard_map/layer/pallas_call | solution.py:569
  104.9 1.5 %copy.17 = bf16[512,64]{0,1:T(8,128)(2,1)} copy(bf16[512,64]{0,1:T(8,128)(2,1)} %bitcast.8) | data formatting | bytes 131072
  106.4 1.5 %copy.18 = bf16[512,64]{0,1:T(8,128)(2,1)} copy(bf16[512,64]{0,1:T(8,128)(2,1)} %bitcast.7) | data formatting | bytes 131072

commit v3 on v2

--- a/solution.py
+++ b/solution.py
@@ -19,10 +19,11 @@
 NT = (((1,), (1,)), ((), ()))
 
 GATHER_LANES = ((0, 384), (384, 384), (768, 256))
-GATHER_ORDER = ("zxy", "yzx", "xyz")
+GATHER_ORDER = ("xzy", "yzx", "xyz")
 SCATTER_ROWS = ((0, 96), (96, 96), (192, 64))
-SCATTER_ORDER = ("yzx", "zxy", "xyz")
+SCATTER_ORDER = ("zyx", "xyz", "yzx")
 BESIDE = (0, -1, 1, 2)
+GROUPS = (2, -1, 1, 0)
 
 
 def device_at(x, y, z, c):
@@ -51,6 +52,19 @@
     return index
 
 
+def kept_block(where, kept):
+    index = ()
+    if "x" in kept:
+        index += (slice(None) if where["x"] is None else where["x"] % 2,)
+    if "z" in kept:
+        index += (slice(None) if where["z"] is None else where["z"],)
+    if "x" in kept:
+        index += (slice(None) if where["x"] is None else where["x"] // 2,)
+    if "y" in kept:
+        index += (slice(None) if where["y"] is None else where["y"],)
+    return index
+
+
 def kept_shape(kept):
     shape = ()
     if "x" in kept:
@@ -75,9 +89,9 @@
     *rest,
 ):
     landing = [[rest[k * 3 + s] for s in range(3)] for k in range(3)]
-    transit = [[rest[9 + k * 3 + s] for s in range(3)] for k in range(3)]
+    transit = [[rest[9 + k * 2 + s] for s in range(2)] for k in range(3)]
     (kv_sem, load_sem, swap_s, swap_r, att_s, att_r, gain_s, gain_r, proj_s, proj_r,
-     ga_s, ga_r, sc_s, sc_r, fin_s, fin_r) = rest[18:]
+     ga_s, ga_r, sc_s, sc_r, fin_s, fin_r) = rest[15:]
 
     g = lax.axis_index("grp")
     h = lax.axis_index("head")
@@ -120,33 +134,6 @@
     for t in range(4):
         gain_own[t:t + 1, :] = gain[:, t * 128:(t + 1) * 128].astype(F32)
     gain_own[4:8, :] = jnp.zeros((4, 128), F32)
-    pl.semaphore_wait(barrier, len(partners))
-
-    swaps = []
-    for i, (src, dst) in enumerate(
-        ((out_w, ow_sib), (resid, resid_sib), (gate_w, gate_up.at[pl.ds(HID, HID)]),
-         (up_w, gate_up.at[pl.ds(3 * HID, HID)]), (down_w, down_all.at[pl.ds(HID, HID)]))
-    ):
-        copy = pltpu.make_async_remote_copy(
-            src_ref=src, dst_ref=dst, send_sem=swap_s.at[i], recv_sem=swap_r.at[i],
-            device_id=sibling, device_id_type=MESH,
-        )
-        copy.start()
-        swaps.append(copy)
-    gain_copies = []
-    for i in range(1, 16):
-        copy = pltpu.make_async_remote_copy(
-            src_ref=gain_own,
-            dst_ref=gains.at[g],
-            send_sem=gain_s.at[i - 1],
-            recv_sem=gain_r.at[i - 1],
-            device_id=((g + i) % 16, h),
-            device_id_type=MESH,
-        )
-        copy.start()
-        gain_copies.append(copy)
-    gains[g] = gain_own[...]
-
     spot_lane = lax.broadcasted_iota(jnp.int32, (PER_KV, CTX), 1)
 
     def attend(step, _):
@@ -155,24 +142,36 @@
             ring = row % RING
             for copy in cache_copies(row, ring):
                 copy.wait()
-        for u in range(UNROLL):
-            row = step * UNROLL + u
-            ring = row % RING
-            head = heads[row]
-            scores = lax.dot_general(
-                head.astype(BF16), key_ring[ring], NT, preferred_element_type=F32
+        group = [step * UNROLL + u for u in range(UNROLL)]
+        query_rows = [heads[row] for row in group]
+        scores = [
+            lax.dot_general(
+                head.astype(BF16), key_ring[row % RING], NT, preferred_element_type=F32
             ) * HD ** (-0.5)
-            own = jnp.sum(head * new_key_f[pl.ds(row, 1), :], axis=1, keepdims=True) * HD ** (-0.5)
-            live = spot_lane < lengths[row]
-            scores = jnp.where(live, scores, -1e30)
-            top = jnp.maximum(jnp.max(scores, axis=1, keepdims=True), own)
-            weights = jnp.where(live, jnp.exp(scores - top), 0.0)
-            own = jnp.exp(own - top)
-            share = 1.0 / (jnp.sum(weights, axis=1, keepdims=True) + own)
-            weights = (weights * share).astype(BF16)
-            own = (own * share).astype(BF16).astype(F32)
-            result = jnp.dot(weights, value_ring[ring], preferred_element_type=F32)
-            mixed[row] = result + own * new_value_f[pl.ds(row, 1), :]
+            for row, head in zip(group, query_rows)
+        ]
+        own = [
+            jnp.sum(head * new_key_f[pl.ds(row, 1), :], axis=1, keepdims=True) * HD ** (-0.5)
+            for row, head in zip(group, query_rows)
+        ]
+        scores = [
+            jnp.where(spot_lane < lengths[row], part, -1e30) for row, part in zip(group, scores)
+        ]
+        tops = [
+            jnp.maximum(jnp.max(part, axis=1, keepdims=True), alone) for part, alone in zip(scores, own)
+        ]
+        weights = [jnp.exp(part - top) for part, top in zip(scores, tops)]
+        own = [jnp.exp(alone - top) for alone, top in zip(own, tops)]
+        shares = [
+            1.0 / (jnp.sum(part, axis=1, keepdims=True) + alone) for part, alone in zip(weights, own)
+        ]
+        results = [
+            jnp.dot((part * share).astype(BF16), value_ring[row % RING], preferred_element_type=F32)
+            + (alone * share).astype(BF16).astype(F32) * new_value_f[pl.ds(row, 1), :]
+            for row, part, alone, share in zip(group, weights, own, shares)
+        ]
+        for row, result in zip(group, results):
+            mixed[row] = result
         for u in range(UNROLL):
             row = step * UNROLL + u
             ring = row % RING
@@ -183,11 +182,27 @@
                     copy.start()
         return 0
 
+    swap_list = (
+        (out_w, ow_sib), (resid, resid_sib), (gate_w, gate_up.at[pl.ds(HID, HID)]),
+        (up_w, gate_up.at[pl.ds(3 * HID, HID)]), (down_w, down_all.at[pl.ds(HID, HID)]),
+    )
+    swaps = []
+
+    def swap(i):
+        copy = pltpu.make_async_remote_copy(
+            src_ref=swap_list[i][0], dst_ref=swap_list[i][1], send_sem=swap_s.at[i], recv_sem=swap_r.at[i],
+            device_id=sibling, device_id_type=MESH,
+        )
+        copy.start()
+        swaps.append(copy)
+
     att_copies = []
     half = SLOTS // 2
     for part in range(2):
         steps = half // UNROLL
         lax.fori_loop(part * steps, (part + 1) * steps, attend, 0)
+        if part == 0:
+            pl.semaphore_wait(barrier, len(partners))
         rows = pl.ds(part * half, half)
         for j in range(PER_KV):
             got_att[xh * 4 + y, rows, j * HD:(j + 1) * HD] = mixed[rows, j, :].astype(BF16)
@@ -203,6 +218,24 @@
             )
             copy.start()
             att_copies.append((i, copy))
+        if part == 0:
+            swap(0)
+            swap(1)
+    for i in range(2, 5):
+        swap(i)
+    gain_copies = []
+    for i in range(1, 16):
+        copy = pltpu.make_async_remote_copy(
+            src_ref=gain_own,
+            dst_ref=gains.at[g],
+            send_sem=gain_s.at[i - 1],
+            recv_sem=gain_r.at[i - 1],
+            device_id=((g + i) % 16, h),
+            device_id_type=MESH,
+        )
+        copy.start()
+        gain_copies.append(copy)
+    gains[g] = gain_own[...]
     loads = []
     for i, (src, dst) in enumerate(
         ((out_w, ow_own), (resid, resid_own), (gate_w, gate_up.at[pl.ds(0, HID)]),
@@ -294,10 +327,11 @@
 
     def gather_copy(k, s, q, which):
         shift, rows, step = (
-            (0, pl.ds(0, 32), 1), (0, pl.ds(0, 32), -1), (-1, pl.ds(0, 16), 1), (1, pl.ds(16, 16), -1)
+            (0, pl.ds(0, 32), 1), (0, pl.ds(0, 32), -1), (-1, pl.ds(0, 16), 1), (1, pl.ds(16, 16), -1),
+            (0, pl.ds(0, 32), 2),
         )[which]
         region = xs.at[(*block_index(gather_spot(k, s, q, shift)), rows, pl.ds(*GATHER_LANES[k]))]
-        index = 4 * (s + q) + which
+        index = 4 * (s + q) + (2 if which == 4 else which)
         copy = pltpu.make_async_remote_copy(
             src_ref=region, dst_ref=region, send_sem=ga_s.at[k, index], recv_sem=ga_r.at[k, index],
             device_id=at(on_axis(GATHER_ORDER[k][s], step), c), device_id_type=MESH,
@@ -328,15 +362,17 @@
             proj_copy(k, head).wait_recv()
             total = total + proj_got[head, :, lanes].astype(F32)
         xs[(*mine, slice(None), lanes)] = total.astype(BF16)
+        gather_copy(k, 0, 0, 4)
         direct(k, 0, 0)
     for k in range(3):
-        forward(k, 0, 0)
-    for k in range(3):
-        finish(k, 0, 0)
+        for which in (0, 1, 4):
+            gathers[k, 0, 0, which].wait_recv()
         direct(k, 1, 0)
+    for k in range(3):
         direct(k, 2, 0)
     for k in range(3):
         forward(k, 1, 0)
+    for k in range(3):
         direct(k, 2, 1)
         direct(k, 2, 2)
     for k in range(3):
@@ -407,6 +443,113 @@
     hidden[...] = (gate * jax.nn.sigmoid(gate) * up).T.astype(BF16)
 
     lane_low = lax.broadcasted_iota(jnp.int32, (256, 128), 1) < 64
+    loads[4].wait()
+    swaps[4].wait()
+
+    scatters = {}
+
+    def halves(k):
+        start, count = SCATTER_ROWS[k]
+        return ((start, count // 2), (start + count // 2, count // 2))
+
+    def scatter_place(k, s, q, shift):
+        order = SCATTER_ORDER[k]
+        place = dict(me)
+        if s == 0:
+            place[order[1]] = (me[order[1]] + GROUPS[q] + 4) % 4
+        place[order[s]] = (me[order[s]] + shift + 4) % 4
+        if s < 2:
+            place[order[2]] = None
+        return place
+
+    def scatter_copy(k, s, q, which):
+        target, part, step = ((2, 0, 1), (2, 1, -1), (1, 1, 1), (-1, 0, -1), (1, 0, 1), (-1, 1, -1))[which]
+        start, count = halves(k)[part]
+        place = scatter_place(k, s, q, target)
+        spot = kept_block(place, SCATTER_ORDER[k][s + 1:])
+        if which < 2:
+            dst = transit[k][s].at[(which, *spot)]
+        else:
+            side = 0 if step == 1 else 1
+            dst = landing[k][s].at[(side, *spot, pl.ds(start - SCATTER_ROWS[k][0], count))]
+        index = 24 * s + 6 * q + which
+        copy = pltpu.make_async_remote_copy(
+            src_ref=ys.at[(*block_index(place), pl.ds(start, count))],
+            dst_ref=dst, send_sem=sc_s.at[k, index], recv_sem=sc_r.at[k, index],
+            device_id=at(on_axis(SCATTER_ORDER[k][s], step), c), device_id_type=MESH,
+        )
+        copy.start()
+        scatters[k, s, q, which] = copy
+
+    def each_block(k, s, q, shift, body):
+        order = SCATTER_ORDER[k]
+
+        def one(block, _):
+            place = scatter_place(k, s, q, shift)
+            place[order[2]] = block
+            body(block_index(place), kept_index(place, order[s + 1:]))
+            return 0
+
+        lax.fori_loop(0, 4, one, 0)
+
+    def scatter_pass(k, s, q):
+        for which, shift in ((0, 1), (1, -1)):
+            scatters[k, s, q, which].wait_recv()
+            rows = pl.ds(*halves(k)[which])
+
+            def add(spot, kept_spot, which=which, rows=rows):
+                both = ys[(*spot, rows)].astype(F32) + transit[k][s][(which, *kept_spot)].astype(F32)
+                ys[(*spot, rows)] = both.astype(BF16)
+
+            each_block(k, s, q, shift, add)
+            scatter_copy(k, s, q, 4 + which)
+
+    def scatter_end(k, s, q):
+        for which in range(2, 6):
+            scatters[k, s, q, which].wait_recv()
+        rows = pl.ds(*SCATTER_ROWS[k])
+
+        def add(spot, kept_spot):
+            sums = ys[(*spot, rows)].astype(F32)
+            for side in range(2):
+                sums = sums + landing[k][s][(side, *kept_spot)].astype(F32)
+            ys[(*spot, rows)] = sums.astype(BF16)
+
+        each_block(k, s, q, 0, add)
+
+    def last_copy(k, d):
+        start, count = SCATTER_ROWS[k]
+        axis = SCATTER_ORDER[k][2]
+        copy = pltpu.make_async_remote_copy(
+            src_ref=ys.at[(*block_index(on_axis(axis, d)), pl.ds(start, count))],
+            dst_ref=landing[k][2].at[d - 1], send_sem=sc_s.at[k, 29 + d], recv_sem=sc_r.at[k, 29 + d],
+            device_id=at(on_axis(axis, d), c), device_id_type=MESH,
+        )
+        copy.start()
+        scatters[k, 2, 0, d] = copy
+
+    for q in range(4):
+        by = (y + GROUPS[q] + 4) % 4
+
+        def project(bxh, _, by=by):
+            col = pl.ds(pl.multiple_of((bxh * 4 + by) * 1024, 1024), 1024)
+            wide = jnp.dot(hidden[...], down_all[:, col], preferred_element_type=F32)
+            for pair in range(4):
+                low = wide[:, pair * 128:(pair + 1) * 128]
+                high = wide[:, 512 + pair * 128:512 + (pair + 1) * 128]
+                first = jnp.where(lane_low, low, pltpu.roll(high, 64, 1)).astype(BF16)
+                second = jnp.where(lane_low, pltpu.roll(low, 64, 1), high).astype(BF16)
+                ys[pair // 2, (pair % 2) * 2, bxh, by] = first
+                ys[pair // 2, (pair % 2) * 2 + 1, bxh, by] = second
+            return 0
+
+        lax.fori_loop(0, 2, project, 0)
+        for which in range(4):
+            scatter_copy(0, 0, q, which)
+            scatter_copy(1, 0, q, which)
+        for part in range(4):
+            for which in ((0, 1), (3,), (2,), ())[q]:
+                scatter_copy(2, 0, part, which)
     odd = h % 2
     tiles = []
     for core in range(2):
@@ -422,137 +565,61 @@
     )
     res_copy.start()
 
-    loads[4].wait()
-    swaps[4].wait()
-
-    def project(block, _):
-        bxh, by = block // 4, block % 4
-        col = pl.ds(pl.multiple_of(block * 1024, 1024), 1024)
-        wide = jnp.dot(hidden[...], down_all[:, col], preferred_element_type=F32)
-        for pair in range(4):
-            low = wide[:, pair * 128:(pair + 1) * 128]
-            high = wide[:, 512 + pair * 128:512 + (pair + 1) * 128]
-            first = jnp.where(lane_low, low, pltpu.roll(high, 64, 1)).astype(BF16)
-            second = jnp.where(lane_low, pltpu.roll(low, 64, 1), high).astype(BF16)
-            ys[pair // 2, (pair % 2) * 2, bxh, by] = first
-            ys[pair // 2, (pair % 2) * 2 + 1, bxh, by] = second
-        return 0
-
-    lax.fori_loop(0, 8, project, 0)
-
-    scatters = {}
-
-    def halves(k):
+    for k in range(3):
+        scatter_pass(k, 0, 0)
+    for k in range(3):
+        scatter_pass(k, 0, 1)
+    for k in range(3):
+        scatter_end(k, 0, 0)
+        scatter_copy(k, 1, 0, 0)
+        scatter_copy(k, 1, 0, 1)
+    for k in range(3):
+        scatter_pass(k, 0, 2)
+    for k in range(3):
+        scatter_end(k, 0, 1)
+        scatter_copy(k, 1, 0, 3)
+    for k in range(3):
+        scatter_pass(k, 0, 3)
+    for k in range(3):
+        scatter_end(k, 0, 2)
+        scatter_copy(k, 1, 0, 2)
+    for k in range(3):
+        scatter_pass(k, 1, 0)
+    for k in range(3):
+        scatter_end(k, 0, 3)
+    for k in range(3):
+        scatter_end(k, 1, 0)
+        for d in (2, 1, 3):
+            last_copy(k, d)
+    for k in range(3):
+        for i in range(1, 8):
+            proj_copy(k, (h + i) % 8).wait_send()
+    for copy in gathers.values():
+        copy.wait_send()
+
+    def give(i, copy, z_ref, out):
+        copy.wait_send()
+        copy.wait_recv()
+        ordered = jnp.dot(perm[...], z_ref[...].reshape(512, 128), preferred_element_type=F32)
+        ordered = jnp.where(c == 0, ordered, pltpu.roll(ordered, 64, 1))
+        out[...] = ordered.T[0:64, :].astype(BF16)
+
+    give(0, res_copy, res_z, res_out)
+    for k in range(3):
         start, count = SCATTER_ROWS[k]
-        return ((start, count // 2), (start + count // 2, count // 2))
-
-    def scatter_place(k, s, shift):
-        order = SCATTER_ORDER[k]
-        place = dict(me)
-        place[order[s]] = (me[order[s]] + shift + 4) % 4
-        for a in order[s + 1:]:
-            place[a] = None
-        return place
-
-    def scatter_copy(k, s, which):
-        target, part, step = ((2, 0, 1), (2, 1, -1), (1, 1, 1), (-1, 0, -1), (1, 0, 1), (-1, 1, -1))[which]
-        start, count = halves(k)[part]
-        if which < 2:
-            dst = transit[k][s].at[which]
-        else:
-            side = 0 if step == 1 else 1
-            everything = (slice(None),) * len(kept_shape(SCATTER_ORDER[k][s + 1:]))
-            dst = landing[k][s].at[(side, *everything, pl.ds(start - SCATTER_ROWS[k][0], count))]
-        copy = pltpu.make_async_remote_copy(
-            src_ref=ys.at[(*block_index(scatter_place(k, s, target)), pl.ds(start, count))],
-            dst_ref=dst, send_sem=sc_s.at[k, s, which], recv_sem=sc_r.at[k, s, which],
-            device_id=at(on_axis(SCATTER_ORDER[k][s], step), c), device_id_type=MESH,
-        )
-        copy.start()
-        scatters[k, s, which] = copy
-
-    def each_block(k, s, shift, body):
-        kept = SCATTER_ORDER[k][s + 1:]
-
-        def one(block, _):
-            place = scatter_place(k, s, shift)
-            for i, a in enumerate(kept):
-                place[a] = (block // 4**i) % 4
-            body(block_index(place), kept_index(place, kept))
-            return 0
-
-        if kept:
-            lax.fori_loop(0, 4 ** len(kept), one, 0)
-        else:
-            one(0, 0)
-
-    def scatter_begin(k, s):
-        for which in range(4):
-            scatter_copy(k, s, which)
-
-    def scatter_pass(k, s):
-        for which, shift in ((0, 1), (1, -1)):
-            scatters[k, s, which].wait_recv()
-            rows = pl.ds(*halves(k)[which])
-
-            def add(spot, kept_spot, which=which, rows=rows):
-                both = ys[(*spot, rows)].astype(F32) + transit[k][s][(which, *kept_spot)].astype(F32)
-                ys[(*spot, rows)] = both.astype(BF16)
-
-            each_block(k, s, shift, add)
-            scatter_copy(k, s, 4 + which)
-
-    def scatter_end(k, s):
-        for which in range(2, 6):
-            scatters[k, s, which].wait_recv()
-        start, count = SCATTER_ROWS[k]
-        rows = pl.ds(start, count)
-
-        def add(spot, kept_spot):
-            sums = ys[(*spot, rows)].astype(F32)
-            for side in range(2):
-                sums = sums + landing[k][s][(side, *kept_spot)].astype(F32)
-            sums = sums.astype(BF16)
-            if s < 2:
-                ys[(*spot, rows)] = sums
-            else:
-                lay_z[start // 32:(start + count) // 32, c] = sums.reshape(count // 32, 32, 128)
-
-        each_block(k, s, 0, add)
-
-    for k in range(3):
-        scatter_begin(k, 0)
-    for s in range(3):
-        for k in range(3):
-            scatter_pass(k, s)
-        for k in range(3):
-            scatter_end(k, s)
-            if s < 2:
-                scatter_begin(k, s + 1)
-
+        sums = ys[(*block_index(me), pl.ds(start, count))].astype(F32)
+        for d in range(1, 4):
+            scatters[k, 2, 0, d].wait_recv()
+            sums = sums + landing[k][2][d - 1].astype(F32)
+        lay_z[start // 32:(start + count) // 32, c] = sums.astype(BF16).reshape(count // 32, 32, 128)
     lay_copy = pltpu.make_async_remote_copy(
         src_ref=lay_z.at[:, c], dst_ref=lay_z.at[:, c], send_sem=fin_s.at[1], recv_sem=fin_r.at[1],
         device_id=sibling, device_id_type=MESH,
     )
     lay_copy.start()
-    for k in range(3):
-        for i in range(1, 8):
-            proj_copy(k, (h + i) % 8).wait_send()
-    for copy in gathers.values():
-        copy.wait_send()
     for copy in scatters.values():
         copy.wait_send()
-
-    for i, (copy, z_ref, out) in enumerate(((res_copy, res_z, res_out), (lay_copy, lay_z, lay_out))):
-        copy.wait_send()
-        pltpu.make_async_remote_copy(
-            src_ref=z_ref.at[:, 1 - c], dst_ref=z_ref.at[:, 1 - c],
-            send_sem=fin_s.at[i], recv_sem=fin_r.at[i],
-            device_id=sibling, device_id_type=MESH,
-        ).wait_recv()
-        ordered = jnp.dot(perm[...], z_ref[...].reshape(512, 128), preferred_element_type=F32)
-        ordered = jnp.where(c == 0, ordered, pltpu.roll(ordered, 64, 1))
-        out[...] = ordered.T[0:64, :].astype(BF16)
+    give(1, lay_copy, lay_z, lay_out)
 
 
 def layer(query, new_key, new_value, lengths, gain, slots, *hbm_args):
@@ -564,8 +631,9 @@
     for k in range(3):
         for s in range(3):
             kept, count = kept_shape(SCATTER_ORDER[k][s + 1:]), SCATTER_ROWS[k][1]
-            landing.append(pltpu.VMEM((2, *kept, count, 128), BF16))
-            transit.append(pltpu.VMEM((2, *kept, count // 2, 128), BF16))
+            landing.append(pltpu.VMEM((3 if s == 2 else 2, *kept, count, 128), BF16))
+            if s < 2:
+                transit.append(pltpu.VMEM((2, *kept, count // 2, 128), BF16))
     return pl.pallas_call(
         layer_kernel,
         out_shape=[jax.ShapeDtypeStruct((64, 512), BF16)] * 2,
@@ -608,7 +676,7 @@
             dma((15,)), dma((15,)),
             dma((3, 8)), dma((3, 8)),
             dma((3, 24)), dma((3, 24)),
-            dma((3, 3, 6)), dma((3, 3, 6)),
+            dma((3, 33)), dma((3, 33)),
             dma((2,)), dma((2,)),
         ],
         compiler_params=pltpu.CompilerParams(

time: 108 us -> 92.3 us (0.85)
  Pallas kernels: 103 us -> 87.1 us
    pallas_call x1, Pallas kernels: 103 us -> 87.1 us  [layer(): pl.pallas_call(layer_kernel, out_shape=[jax.ShapeDtypeStruct((64, 512), B...]
where the time goes in v3:
time: 92.3 us; the launch traced here: 91.9 us
  Pallas kernels  87.1 us (94%)
  local copies, waits for them, and re-layouts  4.21 us (5%)
    pallas_call x1, Pallas kernels, layer(): pl.pallas_call(layer_kernel, out_shape=[jax.ShapeDtypeStruct((64, 512), B...  87.1 us
    unnamed x2, local copies, waits for them, and re-layouts  2.95 us

profile of v3, /device:TPU:1, one launch (start us, length us, event | category | flops | bytes accessed | tf_op | source)
XLA Modules:
  0.0 91.9 jit_solution(16673571439286929067)
XLA Ops:
  0.6 1.3 %broadcast_in_dim.6.gain = bf16[1,512]{1,0:T(2,128)(2,1)} reshape(bf16[512]{0:T(512)(128)(2,1)} %param.22) | data formatting | bytes 2048 | tf_op jit(solution)/shard_map/broadcast_in_dim | solution.py:706
  1.9 87.1 %layer.1 = (bf16[64,512]{1,0:T(8,128)(2,1)}, bf16[64,512]{1,0:T(8,128)(2,1)}) custom-call(bf16[32,1024]{1,0:T(8,128)(2,1)} %query.1, bf16[32,128]{1,0:T(8,128)(2,1)} %new_key.1, bf16[32,128]{1,0:T(8,128)(2,1)} %new_value.1, s32[32]{0:T(128)} %lengths.1, bf16[1,512]{1,0:T(2,128)(2,1)} %broadcast_in_dim.6.gain, s32[1,512]{1,0:T(1,128)} %bitcast.9, ...), custom_call_target="tpu_custom_call" | custom-call | flops 6000000000 | bytes 42000000 | tf_op jit(solution)/shard_map/layer/pallas_call | solution.py:637
  89.0 1.5 %copy.17 = bf16[512,64]{0,1:T(8,128)(2,1)} copy(bf16[512,64]{0,1:T(8,128)(2,1)} %bitcast.8) | data formatting | bytes 131072
  90.4 1.5 %copy.18 = bf16[512,64]{0,1:T(8,128)(2,1)} copy(bf16[512,64]{0,1:T(8,128)(2,1)} %bitcast.7) | data formatting | bytes 131072

commit v4 on v3

--- a/solution.py
+++ b/solution.py
@@ -80,8 +80,8 @@
 
 def layer_kernel(
     query, new_key, new_value, lengths, gain, slots, keys, values, resid, out_w, gate_w, up_w, down_w,
-    res_out, lay_out,
-    key_ring, value_ring, heads, mixed, new_key_f, new_value_f,
+    both_out,
+    key_ring, value_ring, score_ring, heads, mixed, new_key_f, new_value_f,
     gain_own, gains, got_att, resid_own, resid_sib, ow_own, ow_sib,
     gate_up, down_all,
     proj, proj_got, xs, ys, acc, square,
@@ -131,31 +131,36 @@
     new_value_f[...] = new_value[...].astype(F32)
     for j in range(PER_KV):
         heads[:, j, :] = query[:, j * HD:(j + 1) * HD].astype(F32)
-    for t in range(4):
-        gain_own[t:t + 1, :] = gain[:, t * 128:(t + 1) * 128].astype(F32)
+    gain_own[0:4, :] = gain[...].astype(F32)
     gain_own[4:8, :] = jnp.zeros((4, 128), F32)
     spot_lane = lax.broadcasted_iota(jnp.int32, (PER_KV, CTX), 1)
 
-    def attend(step, _):
-        for u in range(UNROLL):
-            row = step * UNROLL + u
-            ring = row % RING
-            for copy in cache_copies(row, ring):
-                copy.wait()
-        group = [step * UNROLL + u for u in range(UNROLL)]
-        query_rows = [heads[row] for row in group]
-        scores = [
-            lax.dot_general(
+    def rows_of(step):
+        return [step * UNROLL + u for u in range(UNROLL)]
+
+    def refill(which, step):
+        for row in rows_of(step):
+
+            @pl.when(row + RING < SLOTS)
+            def _():
+                cache_copies(row + RING, row % RING)[which].start()
+
+    def score(step):
+        found = []
+        for row in rows_of(step):
+            head = heads[row]
+            part = lax.dot_general(
                 head.astype(BF16), key_ring[row % RING], NT, preferred_element_type=F32
             ) * HD ** (-0.5)
-            for row, head in zip(group, query_rows)
-        ]
+            found.append(jnp.where(spot_lane < lengths[row], part, -1e30))
+        return found
+
+    def mix(step):
+        group = rows_of(step)
+        scores = [score_ring[step % 2, u] for u in range(UNROLL)]
         own = [
-            jnp.sum(head * new_key_f[pl.ds(row, 1), :], axis=1, keepdims=True) * HD ** (-0.5)
-            for row, head in zip(group, query_rows)
-        ]
-        scores = [
-            jnp.where(spot_lane < lengths[row], part, -1e30) for row, part in zip(group, scores)
+            jnp.sum(heads[row] * new_key_f[pl.ds(row, 1), :], axis=1, keepdims=True) * HD ** (-0.5)
+            for row in group
         ]
         tops = [
             jnp.maximum(jnp.max(part, axis=1, keepdims=True), alone) for part, alone in zip(scores, own)
@@ -165,23 +170,31 @@
         shares = [
             1.0 / (jnp.sum(part, axis=1, keepdims=True) + alone) for part, alone in zip(weights, own)
         ]
-        results = [
+        return [
             jnp.dot((part * share).astype(BF16), value_ring[row % RING], preferred_element_type=F32)
             + (alone * share).astype(BF16).astype(F32) * new_value_f[pl.ds(row, 1), :]
             for row, part, alone, share in zip(group, weights, own, shares)
         ]
-        for row, result in zip(group, results):
+
+    def attend(step, _):
+        for row in rows_of(step + 1):
+            cache_copies(row, row % RING)[0].wait()
+        for row in rows_of(step):
+            cache_copies(row, row % RING)[1].wait()
+        coming = score(step + 1)
+        for row, result in zip(rows_of(step), mix(step)):
             mixed[row] = result
         for u in range(UNROLL):
-            row = step * UNROLL + u
-            ring = row % RING
-
-            @pl.when(row + RING < SLOTS)
-            def _():
-                for copy in cache_copies(row + RING, ring):
-                    copy.start()
+            score_ring[(step + 1) % 2, u] = coming[u]
+        refill(0, step + 1)
+        refill(1, step)
         return 0
 
+    for row in rows_of(0):
+        cache_copies(row, row % RING)[0].wait()
+    for u, first in enumerate(score(0)):
+        score_ring[0, u] = first
+    refill(0, 0)
     swap_list = (
         (out_w, ow_sib), (resid, resid_sib), (gate_w, gate_up.at[pl.ds(HID, HID)]),
         (up_w, gate_up.at[pl.ds(3 * HID, HID)]), (down_w, down_all.at[pl.ds(HID, HID)]),
@@ -200,7 +213,13 @@
     half = SLOTS // 2
     for part in range(2):
         steps = half // UNROLL
-        lax.fori_loop(part * steps, (part + 1) * steps, attend, 0)
+        lax.fori_loop(part * steps, (part + 1) * steps - part, attend, 0)
+        if part == 1:
+            last = 2 * steps - 1
+            for row in rows_of(last):
+                cache_copies(row, row % RING)[1].wait()
+            for row, result in zip(rows_of(last), mix(last)):
+                mixed[row] = result
         if part == 0:
             pl.semaphore_wait(barrier, len(partners))
         rows = pl.ds(part * half, half)
@@ -481,41 +500,48 @@
         copy.start()
         scatters[k, s, q, which] = copy
 
-    def each_block(k, s, q, shift, body):
+    def each_block(k, s, q, shift):
         order = SCATTER_ORDER[k]
-
-        def one(block, _):
+        found = []
+        for block in range(4):
             place = scatter_place(k, s, q, shift)
             place[order[2]] = block
-            body(block_index(place), kept_index(place, order[s + 1:]))
-            return 0
-
-        lax.fori_loop(0, 4, one, 0)
+            found.append((block_index(place), kept_index(place, order[s + 1:])))
+        return found
 
     def scatter_pass(k, s, q):
         for which, shift in ((0, 1), (1, -1)):
             scatters[k, s, q, which].wait_recv()
             rows = pl.ds(*halves(k)[which])
-
-            def add(spot, kept_spot, which=which, rows=rows):
-                both = ys[(*spot, rows)].astype(F32) + transit[k][s][(which, *kept_spot)].astype(F32)
+            found = each_block(k, s, q, shift)
+            sums = [
+                ys[(*spot, rows)].astype(F32) + transit[k][s][(which, *kept_spot)].astype(F32)
+                for spot, kept_spot in found
+            ]
+            for (spot, _), both in zip(found, sums):
                 ys[(*spot, rows)] = both.astype(BF16)
-
-            each_block(k, s, q, shift, add)
             scatter_copy(k, s, q, 4 + which)
 
     def scatter_end(k, s, q):
         for which in range(2, 6):
             scatters[k, s, q, which].wait_recv()
         rows = pl.ds(*SCATTER_ROWS[k])
-
-        def add(spot, kept_spot):
-            sums = ys[(*spot, rows)].astype(F32)
-            for side in range(2):
-                sums = sums + landing[k][s][(side, *kept_spot)].astype(F32)
-            ys[(*spot, rows)] = sums.astype(BF16)
-
-        each_block(k, s, q, 0, add)
+        found = each_block(k, s, q, 0)
+        sums = [
+            (
+                ys[(*spot, rows)].astype(F32)
+                + landing[k][s][(0, *kept_spot)].astype(F32)
+                + landing[k][s][(1, *kept_spot)].astype(F32)
+            ).astype(BF16)
+            for spot, kept_spot in found
+        ]
+        for (spot, _), both in zip(found, sums):
+            ys[(*spot, rows)] = both
+
+    def near(q):
+        for which in (2, 3):
+            scatter_copy(0, 0, q, which)
+            scatter_copy(1, 0, q, which)
 
     def last_copy(k, d):
         start, count = SCATTER_ROWS[k]
@@ -544,7 +570,7 @@
             return 0
 
         lax.fori_loop(0, 2, project, 0)
-        for which in range(4):
+        for which in range(2):
             scatter_copy(0, 0, q, which)
             scatter_copy(1, 0, q, which)
         for part in range(4):
@@ -565,16 +591,20 @@
     )
     res_copy.start()
 
+    near(0)
     for k in range(3):
         scatter_pass(k, 0, 0)
+    near(1)
     for k in range(3):
         scatter_pass(k, 0, 1)
+    near(2)
     for k in range(3):
         scatter_end(k, 0, 0)
         scatter_copy(k, 1, 0, 0)
         scatter_copy(k, 1, 0, 1)
     for k in range(3):
         scatter_pass(k, 0, 2)
+    near(3)
     for k in range(3):
         scatter_end(k, 0, 1)
         scatter_copy(k, 1, 0, 3)
@@ -597,14 +627,14 @@
     for copy in gathers.values():
         copy.wait_send()
 
-    def give(i, copy, z_ref, out):
+    def give(i, copy, z_ref):
         copy.wait_send()
         copy.wait_recv()
         ordered = jnp.dot(perm[...], z_ref[...].reshape(512, 128), preferred_element_type=F32)
         ordered = jnp.where(c == 0, ordered, pltpu.roll(ordered, 64, 1))
-        out[...] = ordered.T[0:64, :].astype(BF16)
-
-    give(0, res_copy, res_z, res_out)
+        both_out[i] = ordered.T[0:64, :].astype(BF16)
+
+    give(0, res_copy, res_z)
     for k in range(3):
         start, count = SCATTER_ROWS[k]
         sums = ys[(*block_index(me), pl.ds(start, count))].astype(F32)
@@ -619,7 +649,7 @@
     lay_copy.start()
     for copy in scatters.values():
         copy.wait_send()
-    give(1, lay_copy, lay_z, lay_out)
+    give(1, lay_copy, lay_z)
 
 
 def layer(query, new_key, new_value, lengths, gain, slots, *hbm_args):
@@ -636,12 +666,13 @@
                 transit.append(pltpu.VMEM((2, *kept, count // 2, 128), BF16))
     return pl.pallas_call(
         layer_kernel,
-        out_shape=[jax.ShapeDtypeStruct((64, 512), BF16)] * 2,
+        out_shape=jax.ShapeDtypeStruct((2, 64, 512), BF16),
         in_specs=[vmem, vmem, vmem, smem, vmem, vmem] + [hbm] * len(hbm_args),
-        out_specs=[vmem, vmem],
+        out_specs=vmem,
         scratch_shapes=[
             pltpu.VMEM((RING, CTX, HD), BF16),
             pltpu.VMEM((RING, CTX, HD), BF16),
+            pltpu.VMEM((2, UNROLL, PER_KV, CTX), F32),
             pltpu.VMEM((SLOTS, PER_KV, HD), F32),
             pltpu.VMEM((SLOTS, PER_KV, HD), F32),
             pltpu.VMEM((SLOTS, HD), F32),
@@ -702,11 +733,11 @@
     up_weight,
     down_weight,
 ):
-    residual, output = layer(
-        query, new_key, new_value, lengths, norm_gain[None, :], slot_row[None, :],
+    both = layer(
+        query, new_key, new_value, lengths, norm_gain.reshape(4, 128), slot_row[None, :],
         key_cache, value_cache, resid, out_weight, gate_weight.T, up_weight.T, down_weight,
     )
-    return (residual.T, output.T)
+    return (both[0].T, both[1].T)
 
 
 def solution(mesh):

time: 92.3 us -> 89 us (0.964)
  local copies, waits for them, and re-layouts: 4.21 us -> 1.53 us
    unnamed x2 -> x0, local copies, waits for them, and re-layouts: 2.95 us -> none
    transpose x0 -> x1, local copies, waits for them, and re-layouts: none -> 1.53 us  [per_device(): return (both[0].T, both[1].T)]
    broadcast_in_dim x1 -> x0, local copies, waits for them, and re-layouts: 1.26 us -> none  [per_device(): norm_gain[None, :]]
where the time goes in v4:
time: 89 us; the launch traced here: 88.7 us
  Pallas kernels  86.5 us (97%)
  local copies, waits for them, and re-layouts  1.53 us (2%)
    pallas_call x1, Pallas kernels, layer(): pl.pallas_call(layer_kernel, out_shape=jax.ShapeDtypeStruct((2, 64, 512),...  86.5 us

profile of v4, /device:TPU:1, one launch (start us, length us, event | category | flops | bytes accessed | tf_op | source)
XLA Modules:
  0.0 88.7 jit_solution(2514940346058588314)
XLA Ops:
  0.6 86.5 %layer.1 = bf16[2,64,512]{2,1,0:T(8,128)(2,1)} custom-call(bf16[32,1024]{1,0:T(8,128)(2,1)} %query.1, bf16[32,128]{1,0:T(8,128)(2,1)} %new_key.1, bf16[32,128]{1,0:T(8,128)(2,1)} %new_value.1, s32[32]{0:T(128)} %lengths.1, bf16[4,128]{1,0:T(4,128)(2,1)} %bitcast.15, s32[1,512]{1,0:T(1,128)} %bitcast.14, bf16[32,1,1024,128]{3,2,1,0:T(8,128)(2,1)} %keys.1, ...), custom_call_target="tpu_custom_call" | custom-call | flops 6000000000 | bytes 42000000 | tf_op jit(solution)/shard_map/layer/pallas_call | solution.py:667
  87.1 1.5 %slice_bitcast_fusion = (bf16[512,64]{0,1:T(8,128)(2,1)}, bf16[512,64]{0,1:T(8,128)(2,1)}) fusion(bf16[2,64,512]{2,1,0:T(8,128)(2,1)} %layer.1), kind=kLoop, calls=%fused_computation | loop fusion | bytes 262144 | tf_op jit(solution)/shard_map/transpose | solution.py:740

commit v5 on v4

--- a/solution.py
+++ b/solution.py
@@ -386,16 +386,17 @@
     for k in range(3):
         for which in (0, 1, 4):
             gathers[k, 0, 0, which].wait_recv()
+        gather_copy(k, 1, 0, 4)
         direct(k, 1, 0)
     for k in range(3):
         direct(k, 2, 0)
     for k in range(3):
-        forward(k, 1, 0)
-    for k in range(3):
+        gathers[k, 1, 0, 0].wait_recv()
         direct(k, 2, 1)
+        gathers[k, 1, 0, 1].wait_recv()
         direct(k, 2, 2)
     for k in range(3):
-        finish(k, 1, 0)
+        gathers[k, 1, 0, 4].wait_recv()
         direct(k, 2, 3)
 
     def feed(k, blocks):
@@ -406,10 +407,11 @@
             block = bxh * 4 + by
             pieces = []
             for t in range(start // 128, (start + width) // 128):
-                part = xs[:, :, bxh, by, :, t * 128:(t + 1) * 128].reshape(256, 128).astype(F32)
+                part = xs[:, :, bxh, by, :, t * 128:(t + 1) * 128].reshape(256, 128)
+                scale = gains[2 * block + t // 4, t % 4:t % 4 + 1, :].astype(BF16)
+                pieces.append(part * scale)
+                part = part.astype(F32)
                 sums = sums + part * part
-                scale = gains[2 * block + t // 4, t % 4:t % 4 + 1, :]
-                pieces.append((part * scale).astype(BF16))
             scaled = jnp.concatenate(pieces, axis=1)
             depth = pl.ds(pl.multiple_of(block * 1024 + start, 128), width)
             term = lax.dot_general(gate_up[:, depth], scaled, NT, preferred_element_type=F32)

time: 89 us -> 88.8 us (level)
  no operation moved by 1% of the time
where the time goes in v5:
time: 88.8 us; the launch traced here: 88.4 us
  Pallas kernels  86.3 us (97%)
  local copies, waits for them, and re-layouts  1.53 us (2%)
    pallas_call x1, Pallas kernels, layer(): pl.pallas_call(layer_kernel, out_shape=jax.ShapeDtypeStruct((2, 64, 512),...  86.3 us

profile of v5, /device:TPU:1, one launch (start us, length us, event | category | flops | bytes accessed | tf_op | source)
XLA Modules:
  0.0 88.4 jit_solution(17186954628584201848)
XLA Ops:
  0.6 86.3 %layer.1 = bf16[2,64,512]{2,1,0:T(8,128)(2,1)} custom-call(bf16[32,1024]{1,0:T(8,128)(2,1)} %query.1, bf16[32,128]{1,0:T(8,128)(2,1)} %new_key.1, bf16[32,128]{1,0:T(8,128)(2,1)} %new_value.1, s32[32]{0:T(128)} %lengths.1, bf16[4,128]{1,0:T(4,128)(2,1)} %bitcast.15, s32[1,512]{1,0:T(1,128)} %bitcast.14, bf16[32,1,1024,128]{3,2,1,0:T(8,128)(2,1)} %keys.1, ...), custom_call_target="tpu_custom_call" | custom-call | flops 6000000000 | bytes 42000000 | tf_op jit(solution)/shard_map/layer/pallas_call | solution.py:669
  86.9 1.5 %slice_bitcast_fusion = (bf16[512,64]{0,1:T(8,128)(2,1)}, bf16[512,64]{0,1:T(8,128)(2,1)}) fusion(bf16[2,64,512]{2,1,0:T(8,128)(2,1)} %layer.1), kind=kLoop, calls=%fused_computation | loop fusion | bytes 262144 | tf_op jit(solution)/shard_map/transpose | solution.py:742
